TPU v7x, 256 devices: a whole 4x4x8 slice. The times are simulated.
256 devices in a mesh: seq: 8 (over x, z_hi), res: 32 (over z_lo, y, core).
Axes of the slice: x: 4, y: 4, z: 8 (z_hi: 2, z_lo: 4; z = z_hi * 4 + z_lo), core: 2. Of those that a mesh axis runs over, the one named last changes fastest.
Arguments:
- extra_activations: bfloat16 [256, 65536], P('seq', 'res'), may hold values from -6 to 6
- twofold_representation: bfloat16 [1024, 1024, 128], P('res', 'seq'), may hold values from -6 to 6
- present_indicator: int32 [256, 1024], P('seq', 'res'), may hold values 0 or 1
- amino_presence: int32 [1024], P('res'), may hold values 0 or 1
- twofold_offset_matrix: bfloat16 [128, 8], replicated, may hold values from -1.5859375 to 1.5859375
- horizontal_matrix: bfloat16 [64, 256], replicated, may hold values from -8 to 8, as said below
- horizontal_exit_matrix: bfloat16 [64, 64], replicated, may hold values from -1.5 to 1.5
- vertical_matrix: bfloat16 [64, 144], replicated, may hold values from -8 to 8, as said below
- vertical_exit_matrix: bfloat16 [64, 64], replicated, may hold values from -0.75 to 0.75
Outputs:
- msa_out: bfloat16 [256, 65536], P('seq', 'res')
Inputs may be any that keep to these rules, and one draw needn't show every extreme that they name: `horizontal_matrix`: a projection matrix. `vertical_matrix`: a projection matrix.
All inputs are finite; a program needn't handle non-finite values. No bound on the sum of `present_indicator` or of `amino_presence` on one device may be relied on, other than what follows from the above.
Results may differ from a plain program's by a relative error of at most 0.02.
The roundings to bfloat16 on the way count: a program that leaves them out, or rounds other values in their place, can miss the bound.
Values may be sent and summed in bfloat16 or wider, within the bound.
A program may use at most 64 MiB of HBM per device.

v0:
```python
import jax
import jax.numpy as jnp
from jax import lax
from jax.sharding import PartitionSpec as P


def layer_normalize(values_in):
    centre = values_in - jnp.mean(values_in, axis=-1, keepdims=True)
    spread = jnp.mean(centre * centre, axis=-1, keepdims=True)
    return centre * lax.rsqrt(spread + 1e-05)


def complete_column(homolog_line, column_gate, attended_output, vertical_exit_matrix):
    sequence_count, column_count, feature_size = homolog_line.shape
    head_number, head_channel_width = (attended_output.shape[1], attended_output.shape[2])
    hidden_size = head_number * head_channel_width
    gated = (
        jax.nn.sigmoid(column_gate).reshape(
            sequence_count, column_count, head_number, head_channel_width
        )
        * attended_output[None]
    )
    gated = gated.reshape(sequence_count * column_count, hidden_size).astype(jnp.bfloat16)
    horizontal_update = jnp.dot(
        gated, vertical_exit_matrix, preferred_element_type=jnp.float32
    ).reshape(sequence_count, column_count, feature_size)
    return (homolog_line.astype(jnp.float32) + horizontal_update).astype(jnp.bfloat16)


def column_pieces(homolog_line, vertical_matrix, head_number, head_channel_width):
    sequence_count, column_count, feature_size = homolog_line.shape
    hidden_size = head_number * head_channel_width
    column_normalized = layer_normalize(homolog_line.astype(jnp.float32)).astype(jnp.bfloat16)
    mapped_linear = jnp.dot(
        column_normalized.reshape(-1, feature_size),
        vertical_matrix,
        preferred_element_type=jnp.float32,
    )
    mapped_linear = mapped_linear.reshape(sequence_count, column_count, -1)
    return (
        mapped_linear[..., :hidden_size],
        mapped_linear[..., hidden_size : 2 * hidden_size],
        mapped_linear[..., 2 * hidden_size : 2 * hidden_size + head_channel_width],
        mapped_linear[..., 2 * hidden_size + head_channel_width :],
    )


def column_logits(kept_entries, mean_query, column_key, head_number, head_channel_width):
    column_count = mean_query.shape[0]
    logits = jnp.einsum(
        "ihc,sic->sih",
        mean_query.reshape(column_count, head_number, head_channel_width),
        column_key,
    )
    return logits + 1000000000.0 * (kept_entries - 1.0)[..., None]


def column_complete(
    homolog_line,
    kept_entries,
    vertical_matrix,
    vertical_exit_matrix,
    head_number,
    head_channel_width,
):
    column_query, column_gate, column_key, column_value = column_pieces(
        homolog_line, vertical_matrix, head_number, head_channel_width
    )
    query_total = jnp.sum(kept_entries[..., None] * column_query, axis=0)
    kept_count = jnp.sum(kept_entries, axis=0)
    mean_query = query_total / jnp.maximum(kept_count, 1.0)[:, None] * head_channel_width ** (-0.5)
    logits = column_logits(kept_entries, mean_query, column_key, head_number, head_channel_width)
    exped = jnp.exp(logits - jnp.max(logits, axis=0, keepdims=True))
    attended_output = (
        jnp.einsum("sih,sic->ihc", exped, column_value) / jnp.sum(exped, axis=0)[..., None]
    )
    return complete_column(homolog_line, column_gate, attended_output, vertical_exit_matrix)


def on_device(
    extra_activations,
    twofold_representation,
    present_indicator,
    amino_presence,
    twofold_offset_matrix,
    horizontal_matrix,
    horizontal_exit_matrix,
    vertical_matrix,
    vertical_exit_matrix,
):
    homolog_lines, amino_lines = present_indicator.shape
    feature_size = horizontal_matrix.shape[0]
    hidden_size = horizontal_exit_matrix.shape[0]
    head_number = twofold_offset_matrix.shape[1]
    head_channel_width = hidden_size // head_number
    local_lines = extra_activations.reshape(homolog_lines, amino_lines, feature_size)
    kept_entries = (present_indicator * amino_presence[None, :]).astype(jnp.float32)
    standardised = layer_normalize(local_lines.astype(jnp.float32)).astype(jnp.bfloat16)
    mapped_linear = jnp.dot(
        standardised.reshape(-1, feature_size),
        horizontal_matrix,
        preferred_element_type=jnp.float32,
    )
    mapped_linear = mapped_linear.reshape(homolog_lines, amino_lines, 4 * hidden_size)
    queries = (mapped_linear[..., :hidden_size] * head_channel_width ** (-0.5)).astype(jnp.bfloat16)
    query_heads = queries.reshape(homolog_lines, amino_lines, head_number, head_channel_width)
    gating = mapped_linear[..., 3 * hidden_size :]
    pair_normed = layer_normalize(twofold_representation.astype(jnp.float32)).astype(jnp.bfloat16)
    bias_local = jnp.einsum(
        "ikc,ch->hik", pair_normed, twofold_offset_matrix, preferred_element_type=jnp.float32
    )
    bias_panel = lax.all_gather(bias_local.astype(jnp.bfloat16), "seq", axis=2, tiled=True)
    mask_wire = kept_entries.astype(jnp.bfloat16)

    def attend_block(running, key_block, value_block, mask_block, key_start):
        block_size = key_block.shape[1]
        key_heads = key_block.reshape(homolog_lines, block_size, head_number, head_channel_width)
        value_heads = value_block.reshape(
            homolog_lines, block_size, head_number, head_channel_width
        )
        logits = jnp.einsum(
            "sihc,sjhc->hsij", query_heads, key_heads, preferred_element_type=jnp.float32
        )
        bias_block = lax.dynamic_slice_in_dim(bias_panel, key_start, block_size, 2).astype(
            jnp.float32
        )
        logits = (
            logits
            + bias_block[:, None]
            + (1000000000.0 * (mask_block.astype(jnp.float32) - 1.0))[None, :, None, :]
        )
        peak = jnp.maximum(running[0], jnp.max(logits, axis=-1))
        rescale = jnp.exp(running[0] - peak)
        exped = jnp.exp(logits - peak[..., None])
        total = running[1] * rescale + jnp.sum(exped, axis=-1)
        summed = jnp.einsum(
            "hsij,sjhc->hsic",
            exped.astype(jnp.bfloat16),
            value_heads,
            preferred_element_type=jnp.float32,
        )
        return (peak, total, running[2] * rescale[..., None] + summed)

    def attend_piece(running, key_piece, value_piece, mask_piece):
        key_count = key_piece.shape[1]
        block_size = 128

        def one_block(block_index, state):
            offset_rows = block_index * block_size
            return attend_block(
                state,
                lax.dynamic_slice_in_dim(key_piece, offset_rows, block_size, 1),
                lax.dynamic_slice_in_dim(value_piece, offset_rows, block_size, 1),
                lax.dynamic_slice_in_dim(mask_piece, offset_rows, block_size, 1),
                offset_rows,
            )

        return lax.fori_loop(0, key_count // block_size, one_block, running)

    initial = (
        jnp.full((head_number, homolog_lines, amino_lines), -jnp.inf, jnp.float32),
        jnp.zeros((head_number, homolog_lines, amino_lines), jnp.float32),
        jnp.zeros((head_number, homolog_lines, amino_lines, head_channel_width), jnp.float32),
    )
    key_local = mapped_linear[..., hidden_size : 2 * hidden_size].astype(jnp.bfloat16)
    value_local = mapped_linear[..., 2 * hidden_size : 3 * hidden_size].astype(jnp.bfloat16)
    key_piece = (
        lax.all_gather(key_local, "res", axis=1, tiled=True),
        lax.all_gather(value_local, "res", axis=1, tiled=True),
        lax.all_gather(mask_wire, "res", axis=1, tiled=True),
    )
    answer_tuple = attend_piece(initial, key_piece[0], key_piece[1], key_piece[2])
    attended_output = answer_tuple[2] / answer_tuple[1][..., None]
    attended_output = jnp.transpose(attended_output, (1, 2, 0, 3)).reshape(
        homolog_lines, amino_lines, hidden_size
    )
    row_gated = (jax.nn.sigmoid(gating) * attended_output).astype(jnp.bfloat16)
    horizontal_update = jnp.dot(
        row_gated.reshape(-1, hidden_size),
        horizontal_exit_matrix,
        preferred_element_type=jnp.float32,
    )
    homolog_line = (
        local_lines.astype(jnp.float32)
        + horizontal_update.reshape(homolog_lines, amino_lines, feature_size)
    ).astype(jnp.bfloat16)
    moved_rows, moved_mask = (
        lax.all_to_all(homolog_line, "seq", split_axis=1, concat_axis=0, tiled=True),
        lax.all_to_all(mask_wire, "seq", split_axis=1, concat_axis=0, tiled=True),
    )
    updated = column_complete(
        moved_rows,
        moved_mask.astype(jnp.float32),
        vertical_matrix,
        vertical_exit_matrix,
        head_number,
        head_channel_width,
    )
    ultimate_update = lax.all_to_all(updated, "seq", split_axis=0, concat_axis=1, tiled=True)
    return ultimate_update.reshape(homolog_lines, amino_lines * feature_size)


def solution(mesh):
    in_specs = (
        P("seq", "res"),
        P("res", "seq", None),
        P("seq", "res"),
        P("res"),
        P(),
        P(),
        P(),
        P(),
        P(),
    )
    out_specs = P("seq", "res")
    return jax.shard_map(
        on_device, mesh=mesh, in_specs=in_specs, out_specs=out_specs, check_vma=False
    )
```

profile of v0, /device:TPU:32, one launch (start us, length us, event | category | flops | bytes accessed | tf_op | source)
XLA Modules:
  0.0 307.8 jit_solution(7779853007322636180)
XLA Ops:
  6.6 1.2 reshape.181
  8.0 0.4 multiply_reduce_fusion
  8.4 0.7 fusion.69
  9.1 1.0 fusion.68
  10.2 0.7 all-gather.5.cloned.1.call-update
  11.0 0.7 convert_convert_fusion
  11.7 10.0 %all-to-all-start.1 = ((bf16[32,8,4]{0,2,1:T(4,128)(2,1)}), bf16[32,8,4]{0,2,1:T(4,128)(2,1)S(1)}, u32[]{:S(2)}, u32[]{:S(2)}) async-start(bf16[32,8,4]{0,2,1:T(4,128)(2,1)} %bitcast.12), calls=%async_computation.1 | async-start | bytes 16384 | tf_op jit(solution)/shard_map/all_to_all | solution.py:189
  21.7 0.3 convert_reduce_fusion
  22.1 1.3 fusion.18
  23.4 1.5 fusion.22
  24.9 52.8 %all_gather.13 = bf16[8,32,1024]{2,0,1:T(8,128)(2,1)} all-gather(bf16[8,32,128]{2,0,1:T(8,128)(2,1)S(1)} %fusion.22), channel_id=1, replica_groups=mesh['seq'=8,'res'=32] {'seq'}, dimensions={2}, use_global_device_ids=true | all-gather | bytes 589824 | tf_op jit(solution)/shard_map/all_gather | solution.py:112
  77.7 34.6 %all_gather.14 = bf16[32,1024]{0,1:T(8,128)(2,1)S(1)} all-gather(bf16[32,32]{0,1:T(8,128)(2,1)} %convert_convert_fusion), channel_id=1, replica_groups=mesh['seq'=8,'res'=32] {'res'}, dimensions={1}, use_global_device_ids=true | all-gather | bytes 67584 | tf_op jit(solution)/shard_map/all_gather | solution.py:170
  113.0 8.7 %copy.57 = bf16[32,1024,64]{1,2,0:T(8,128)(2,1)} copy(bf16[32,1024,64]{2,1,0:T(8,128)(2,1)} %all-gather.3.cloned.1.call-done) | data formatting | bytes 8388608
  121.7 44.7 %all-gather.5.cloned.1.call-done = bf16[32,1024,64]{2,1,0:T(8,128)(2,1)} async-done(((bf16[32,32,64]{2,1,0:T(8,128)(2,1)}), bf16[32,1024,64]{2,1,0:T(8,128)(2,1)}) %all-gather.5.cloned.1.call-update) | async-done | bytes 4194320 | tf_op jit(solution)/shard_map/all_gather | solution.py:169
  166.4 8.5 %copy.61 = bf16[32,1024,64]{1,2,0:T(8,128)(2,1)} copy(bf16[32,1024,64]{2,1,0:T(8,128)(2,1)} %all-gather.5.cloned.1.call-done) | data formatting | bytes 8388608
  174.9 85.4 %while.20 = (s32[]{:T(128)}, f32[8,32,32]{2,1,0:T(8,128)S(1)}, f32[8,32,32]{2,1,0:T(8,128)S(1)}, f32[8,32,32,8]{2,3,1,0:T(8,128)S(1)}, bf16[32,1024,64]{1,2,0:T(...) while((s32[]{:T(128)}, f32[8,32,32]{2,1,0:T(8,128)S(1)}, ...), condition=%wide.region_7.0_spmd.clone, body=%wide.region_4.0_spmd.clone.sunk | while | flops 45371396 | bytes 34480348 | solution.py:158
  174.9 1.3 dynamic-slice_bitcast_fusion.3
  176.2 0.9 constant_dynamic-slice_fusion.2
  177.1 2.7 fusion.82
  179.9 4.3 %fusion.83 = f32[8,32,32]{2,1,0:T(8,128)S(1)} fusion(f32[8,32,128,32]{2,3,1,0:T(8,128)} %get-tuple-element.387, f32[8,32,32]{2,1,0:T(8,128)S(1)} %select_maximum_fusion.2, f32[32,128]{1,0:T(8,128)S(1)} %add_multiply_fusion.3, f32[8,32,128]{2,1,0:T(8,128)S(1)} %copy_convert_fusion.2), kind=kLoop, calls=%fused_computation.4.clone.1 | loop fusion | flops 4186112 | bytes 4407296 | tf_op jit(solution)/shard_map/while/body/eval_jaxpr/reduce_sum | solution.py:135
  184.2 1.3 fusion.85
  185.6 1.3 dynamic-slice_bitcast_fusion.3
  186.9 0.9 constant_dynamic-slice_fusion.2
  187.8 2.7 fusion.82
  190.5 4.3 %fusion.83 = f32[8,32,32]{2,1,0:T(8,128)S(1)} fusion(f32[8,32,128,32]{2,3,1,0:T(8,128)} %get-tuple-element.387, f32[8,32,32]{2,1,0:T(8,128)S(1)} %select_maximum_fusion.2, f32[32,128]{1,0:T(8,128)S(1)} %add_multiply_fusion.3, f32[8,32,128]{2,1,0:T(8,128)S(1)} %copy_convert_fusion.2), kind=kLoop, calls=%fused_computation.4.clone.1 | loop fusion | flops 4186112 | bytes 4407296 | tf_op jit(solution)/shard_map/while/body/eval_jaxpr/reduce_sum | solution.py:135
  194.9 1.3 fusion.85
  196.3 1.3 dynamic-slice_bitcast_fusion.3
  197.6 0.9 constant_dynamic-slice_fusion.2
  198.4 2.7 fusion.82
  201.2 4.3 %fusion.83 = f32[8,32,32]{2,1,0:T(8,128)S(1)} fusion(f32[8,32,128,32]{2,3,1,0:T(8,128)} %get-tuple-element.387, f32[8,32,32]{2,1,0:T(8,128)S(1)} %select_maximum_fusion.2, f32[32,128]{1,0:T(8,128)S(1)} %add_multiply_fusion.3, f32[8,32,128]{2,1,0:T(8,128)S(1)} %copy_convert_fusion.2), kind=kLoop, calls=%fused_computation.4.clone.1 | loop fusion | flops 4186112 | bytes 4407296 | tf_op jit(solution)/shard_map/while/body/eval_jaxpr/reduce_sum | solution.py:135
  205.6 1.3 fusion.85
  206.9 1.3 dynamic-slice_bitcast_fusion.3
  208.2 0.9 constant_dynamic-slice_fusion.2
  209.1 2.7 fusion.82
  211.9 4.3 %fusion.83 = f32[8,32,32]{2,1,0:T(8,128)S(1)} fusion(f32[8,32,128,32]{2,3,1,0:T(8,128)} %get-tuple-element.387, f32[8,32,32]{2,1,0:T(8,128)S(1)} %select_maximum_fusion.2, f32[32,128]{1,0:T(8,128)S(1)} %add_multiply_fusion.3, f32[8,32,128]{2,1,0:T(8,128)S(1)} %copy_convert_fusion.2), kind=kLoop, calls=%fused_computation.4.clone.1 | loop fusion | flops 4186112 | bytes 4407296 | tf_op jit(solution)/shard_map/while/body/eval_jaxpr/reduce_sum | solution.py:135
  216.3 1.3 fusion.85
  217.6 1.3 dynamic-slice_bitcast_fusion.3
  218.9 0.9 constant_dynamic-slice_fusion.2
  219.8 2.7 fusion.82
  222.6 4.3 %fusion.83 = f32[8,32,32]{2,1,0:T(8,128)S(1)} fusion(f32[8,32,128,32]{2,3,1,0:T(8,128)} %get-tuple-element.387, f32[8,32,32]{2,1,0:T(8,128)S(1)} %select_maximum_fusion.2, f32[32,128]{1,0:T(8,128)S(1)} %add_multiply_fusion.3, f32[8,32,128]{2,1,0:T(8,128)S(1)} %copy_convert_fusion.2), kind=kLoop, calls=%fused_computation.4.clone.1 | loop fusion | flops 4186112 | bytes 4407296 | tf_op jit(solution)/shard_map/while/body/eval_jaxpr/reduce_sum | solution.py:135
  226.9 1.3 fusion.85
  228.3 1.3 dynamic-slice_bitcast_fusion.3
  229.6 0.9 constant_dynamic-slice_fusion.2
  230.5 2.7 fusion.82
  233.2 4.3 %fusion.83 = f32[8,32,32]{2,1,0:T(8,128)S(1)} fusion(f32[8,32,128,32]{2,3,1,0:T(8,128)} %get-tuple-element.387, f32[8,32,32]{2,1,0:T(8,128)S(1)} %select_maximum_fusion.2, f32[32,128]{1,0:T(8,128)S(1)} %add_multiply_fusion.3, f32[8,32,128]{2,1,0:T(8,128)S(1)} %copy_convert_fusion.2), kind=kLoop, calls=%fused_computation.4.clone.1 | loop fusion | flops 4186112 | bytes 4407296 | tf_op jit(solution)/shard_map/while/body/eval_jaxpr/reduce_sum | solution.py:135
  237.6 1.3 fusion.85
  239.0 1.3 dynamic-slice_bitcast_fusion.3
  240.3 0.9 constant_dynamic-slice_fusion.2
  241.2 2.7 fusion.82
  243.9 4.3 %fusion.83 = f32[8,32,32]{2,1,0:T(8,128)S(1)} fusion(f32[8,32,128,32]{2,3,1,0:T(8,128)} %get-tuple-element.387, f32[8,32,32]{2,1,0:T(8,128)S(1)} %select_maximum_fusion.2, f32[32,128]{1,0:T(8,128)S(1)} %add_multiply_fusion.3, f32[8,32,128]{2,1,0:T(8,128)S(1)} %copy_convert_fusion.2), kind=kLoop, calls=%fused_computation.4.clone.1 | loop fusion | flops 4186112 | bytes 4407296 | tf_op jit(solution)/shard_map/while/body/eval_jaxpr/reduce_sum | solution.py:135
  248.3 1.3 fusion.85
  249.6 1.3 dynamic-slice_bitcast_fusion.3
  250.9 0.9 constant_dynamic-slice_fusion.2
  251.8 2.7 fusion.82
  254.6 4.3 %fusion.83 = f32[8,32,32]{2,1,0:T(8,128)S(1)} fusion(f32[8,32,128,32]{2,3,1,0:T(8,128)} %get-tuple-element.387, f32[8,32,32]{2,1,0:T(8,128)S(1)} %select_maximum_fusion.2, f32[32,128]{1,0:T(8,128)S(1)} %add_multiply_fusion.3, f32[8,32,128]{2,1,0:T(8,128)S(1)} %copy_convert_fusion.2), kind=kLoop, calls=%fused_computation.4.clone.1 | loop fusion | flops 4186112 | bytes 4407296 | tf_op jit(solution)/shard_map/while/body/eval_jaxpr/reduce_sum | solution.py:135
  259.0 1.3 fusion.85
  260.8 1.4 fusion.20
  262.3 0.9 reshape.193
  263.2 7.5 %all-to-all-start = ((bf16[8,2,4096]{2,1,0:T(2,128)(2,1)}), bf16[8,2,4096]{2,1,0:T(2,128)(2,1)S(1)}, u32[]{:S(2)}, u32[]{:S(2)}) async-start(bf16[8,2,4096]{2,1,0:T(2,128)(2,1)} %reshape.193), calls=%async_computation | async-start | bytes 262144 | tf_op jit(solution)/shard_map/all_to_all | solution.py:188
  270.8 11.6 %all-to-all-done = bf16[8,2,4096]{2,1,0:T(2,128)(2,1)S(1)} async-done(((bf16[8,2,4096]{2,1,0:T(2,128)(2,1)}), bf16[8,2,4096]{2,1,0:T(2,128)(2,1)S(1)}, u32[]{:S(2)}, u32[]{:S(2)}) %all-to-all-start) | async-done | bytes 131104 | tf_op jit(solution)/shard_map/all_to_all | solution.py:188
  282.9 0.4 fusion.33
  283.7 0.8 fusion.37
  286.1 13.4 %all_to_all.37 = bf16[8,2,4096]{2,1,0:T(2,128)(2,1)S(1)} all-to-all(bf16[8,2,4096]{2,1,0:T(2,128)(2,1)S(1)} %reshape.195), channel_id=1, replica_groups=mesh['seq'=8,'res'=32] {'seq'}, dimensions={0} | all-to-all | bytes 262144 | tf_op jit(solution)/shard_map/all_to_all | solution.py:199
  300.0 0.9 reshape.180
  (122 shorter events, 6.0 us)
Async XLA Ops:
  6.5 1.9 copy-start
  6.5 4.4 %copy-start.5 = (s32[32,32]{1,0:T(8,128)S(1)}, s32[32,32]{1,0:T(8,128)}, u32[]{:S(2)}) copy-start(s32[32,32]{1,0:T(8,128)} %param.13) | copy-start | bytes 12292
  6.5 4.5 %copy-start.6 = (s32[32]{0:T(128)S(1)}, s32[32]{0:T(128)}, u32[]{:S(2)}) copy-start(s32[32]{0:T(128)} %param.14) | copy-start | bytes 388
  6.5 15.2 %copy-start.2 = (bf16[32,128,128]{2,1,0:T(8,128)(2,1)S(1)}, bf16[32,128,128]{2,1,0:T(8,128)(2,1)}, u32[]{:S(2)}) copy-start(bf16[32,128,128]{2,1,0:T(8,128)(2,1)} %param.12) | copy-start | bytes 3145732
  6.5 16.9 %copy-start.9 = (bf16[128,8]{0,1:T(8,128)(2,1)S(1)}, bf16[128,8]{0,1:T(8,128)(2,1)}, u32[]{:S(2)}) copy-start(bf16[128,8]{0,1:T(8,128)(2,1)} %param.15) | copy-start | bytes 6148
  6.5 106.5 %all-gather.3.cloned.1.call-start = ((), (), s32[]{:S(2)}) async-start(), calls=%async_computation.3 | async-start | bytes 8650752 | tf_op jit(solution)/shard_map/all_gather | solution.py:168
  9.1 103.2 %copy-start.3 = (f32[32,32,256]{2,1,0:T(8,128)}, f32[32,32,256]{2,1,0:T(8,128)S(1)}, u32[]{:S(2)}) copy-start(f32[32,32,256]{2,1,0:T(8,128)S(1)} %get-tuple-element.321) | copy-start | bytes 3145732
  10.2 156.2 %all-gather.5.cloned.1.call-start = ((), (), s32[]{:S(2)}) async-start(), calls=%async_computation.4 | async-start | bytes 8650752 | tf_op jit(solution)/shard_map/all_gather | solution.py:169
  11.7 101.2 %all-to-all-start.1 = ((bf16[32,8,4]{0,2,1:T(4,128)(2,1)}), bf16[32,8,4]{0,2,1:T(4,128)(2,1)S(1)}, u32[]{:S(2)}, u32[]{:S(2)}) async-start(bf16[32,8,4]{0,2,1:T(4,128)(2,1)} %bitcast.12), calls=%async_computation.1 | async-start | bytes 16384 | tf_op jit(solution)/shard_map/all_to_all | solution.py:189
  174.9 85.9 %copy-start.7 = (bf16[64,64]{1,0:T(8,128)(2,1)S(1)}, bf16[64,64]{1,0:T(8,128)(2,1)}, u32[]{:S(2)}) copy-start(bf16[64,64]{1,0:T(8,128)(2,1)} %param.17) | copy-start | bytes 24580
  179.8 4.4 %copy-start.1 = (f32[8,32,128,32]{2,3,1,0:T(8,128)S(1)}, f32[8,32,128,32]{2,3,1,0:T(8,128)}, u32[]{:S(2)}) copy-start(f32[8,32,128,32]{2,3,1,0:T(8,128)} %get-tuple-element.387) | copy-start | bytes 12582916 | tf_op jit(solution)/shard_map/while
  190.5 4.4 %copy-start.1 = (f32[8,32,128,32]{2,3,1,0:T(8,128)S(1)}, f32[8,32,128,32]{2,3,1,0:T(8,128)}, u32[]{:S(2)}) copy-start(f32[8,32,128,32]{2,3,1,0:T(8,128)} %get-tuple-element.387) | copy-start | bytes 12582916 | tf_op jit(solution)/shard_map/while
  201.2 4.4 %copy-start.1 = (f32[8,32,128,32]{2,3,1,0:T(8,128)S(1)}, f32[8,32,128,32]{2,3,1,0:T(8,128)}, u32[]{:S(2)}) copy-start(f32[8,32,128,32]{2,3,1,0:T(8,128)} %get-tuple-element.387) | copy-start | bytes 12582916 | tf_op jit(solution)/shard_map/while
  211.9 4.4 %copy-start.1 = (f32[8,32,128,32]{2,3,1,0:T(8,128)S(1)}, f32[8,32,128,32]{2,3,1,0:T(8,128)}, u32[]{:S(2)}) copy-start(f32[8,32,128,32]{2,3,1,0:T(8,128)} %get-tuple-element.387) | copy-start | bytes 12582916 | tf_op jit(solution)/shard_map/while
  222.5 4.4 %copy-start.1 = (f32[8,32,128,32]{2,3,1,0:T(8,128)S(1)}, f32[8,32,128,32]{2,3,1,0:T(8,128)}, u32[]{:S(2)}) copy-start(f32[8,32,128,32]{2,3,1,0:T(8,128)} %get-tuple-element.387) | copy-start | bytes 12582916 | tf_op jit(solution)/shard_map/while
  233.2 4.4 %copy-start.1 = (f32[8,32,128,32]{2,3,1,0:T(8,128)S(1)}, f32[8,32,128,32]{2,3,1,0:T(8,128)}, u32[]{:S(2)}) copy-start(f32[8,32,128,32]{2,3,1,0:T(8,128)} %get-tuple-element.387) | copy-start | bytes 12582916 | tf_op jit(solution)/shard_map/while
  243.9 4.4 %copy-start.1 = (f32[8,32,128,32]{2,3,1,0:T(8,128)S(1)}, f32[8,32,128,32]{2,3,1,0:T(8,128)}, u32[]{:S(2)}) copy-start(f32[8,32,128,32]{2,3,1,0:T(8,128)} %get-tuple-element.387) | copy-start | bytes 12582916 | tf_op jit(solution)/shard_map/while
  254.6 4.4 %copy-start.1 = (f32[8,32,128,32]{2,3,1,0:T(8,128)S(1)}, f32[8,32,128,32]{2,3,1,0:T(8,128)}, u32[]{:S(2)}) copy-start(f32[8,32,128,32]{2,3,1,0:T(8,128)} %get-tuple-element.387) | copy-start | bytes 12582916 | tf_op jit(solution)/shard_map/while
  260.8 22.9 %copy-start.4 = (bf16[64,144]{1,0:T(8,128)(2,1)S(1)}, bf16[64,144]{1,0:T(8,128)(2,1)}, u32[]{:S(2)}) copy-start(bf16[64,144]{1,0:T(8,128)(2,1)} %param.18) | copy-start | bytes 55300
  260.8 24.6 %copy-start.8 = (bf16[64,64]{1,0:T(8,128)(2,1)S(1)}, bf16[64,64]{1,0:T(8,128)(2,1)}, u32[]{:S(2)}) copy-start(bf16[64,64]{1,0:T(8,128)(2,1)} %param.19) | copy-start | bytes 24580
  263.2 19.1 %all-to-all-start = ((bf16[8,2,4096]{2,1,0:T(2,128)(2,1)}), bf16[8,2,4096]{2,1,0:T(2,128)(2,1)S(1)}, u32[]{:S(2)}, u32[]{:S(2)}) async-start(bf16[8,2,4096]{2,1,0:T(2,128)(2,1)} %reshape.193), calls=%async_computation | async-start | bytes 262144 | tf_op jit(solution)/shard_map/all_to_all | solution.py:188
Sparse Core Ops, SparseCore 0:
  10.3 84.8 all-gather.2
  97.1 69.2 all-gather.4
where the time goes:
time: 309 us; the launch traced here: 308 us
  blocking collectives  101 us (33%)
  waiting for transfers between devices  57 us (18%)
  local copies, waits for them, and re-layouts  41.3 us (13%)
  other arithmetic  39.4 us (13%)
  matrix products  37.5 us (12%)
  starting transfers between devices  17.6 us (6%)
  between operations  13.7 us (4%)
    all_gather x1, blocking collectives, on_device(): lax.all_gather(bias_local.astype(jnp.bfloat16), 'seq', axis=2, tiled=True)  52.8 us
    all_gather x1, waiting for transfers between devices, on_device(): lax.all_gather(value_local, 'res', axis=1, tiled=True)  44.7 us
    all_gather x1, blocking collectives, on_device(): lax.all_gather(mask_wire, 'res', axis=1, tiled=True)  34.6 us
    reduce_sum x8, other arithmetic, attend_block(): total = running[1] * rescale + jnp.sum(exped, axis=-1)  34.1 us
    dot_general x8, matrix products, attend_block(): jnp.einsum('sihc,sjhc->hsij', query_heads, key_heads, preferred_element_t...  21.9 us
    unnamed x27, local copies, waits for them, and re-layouts  19.1 us
    all_to_all x1, blocking collectives, on_device(): lax.all_to_all(updated, 'seq', split_axis=0, concat_axis=1, tiled=True)  13.4 us
    all_to_all x1, waiting for transfers between devices, on_device(): lax.all_to_all(homolog_line, 'seq', split_axis=1, concat_axis=0, tiled=True)  11.6 us
  transfers between devices with their start and end apart: 4, of which 2 were waited for; matrix products, arithmetic and copies ran while one was open for 4% of the time, Pallas kernels for 0%

commit v1 on v0

v1 whole, which is shorter than its diff:
```python
import jax
import jax.numpy as jnp
from jax import lax
from jax.experimental import pallas as pl
from jax.experimental.pallas import tpu as pltpu
from jax.sharding import PartitionSpec as P

MESH = pl.DeviceIdType.MESH
F32, BF16 = jnp.float32, jnp.bfloat16
SEQS, RES, PAIRS, LANES = 32, 32, 16, 128
ROWS = PAIRS + SEQS * PAIRS
GROUPS = 4
LOG2E = 1.4426950408889634
SPANS = [
    (0 if g == 0 else PAIRS + g * 128, 128 + (PAIRS if g == 0 else 0)) for g in range(GROUPS)
]


def rows_of(shape):
    return lax.broadcasted_iota(jnp.int32, shape, 0)


def lanes_of(shape):
    return lax.broadcasted_iota(jnp.int32, shape, 1)


def flag(condition):
    return jnp.where(condition, 1.0, 0.0).astype(BF16)


def dot(left, right):
    return jnp.dot(left, right, preferred_element_type=F32)


def dot_nt(left, right):
    return lax.dot_general(left, right, (((1,), (1,)), ((), ())), preferred_element_type=F32)


def dot_split(left, right):
    high = left.astype(BF16)
    low = (left - high.astype(F32)).astype(BF16)
    return dot(high, right) + dot(low, right)


def normalize(values, width):
    shape = (LANES, LANES)
    average = jnp.where(
        rows_of(shape) // width == lanes_of(shape) // width, 1.0 / width, 0.0
    ).astype(BF16)
    centre = values.astype(F32) - dot(values, average)
    spread = dot_split(centre * centre, average)
    return centre * lax.rsqrt(spread + 1e-05)


def tile_rows(weights, shift):
    height, width = weights.shape
    tall = dot(flag(rows_of((LANES, height)) % height == lanes_of((LANES, height))), weights)
    column = rows_of((width, LANES))
    pick = flag(column == lanes_of((width, LANES)) % 64 + shift)
    return dot(tall.astype(BF16), pick)


def twice(weights, shift):
    shape = (LANES, LANES)
    return jnp.where(
        rows_of(shape) // 64 == lanes_of(shape) // 64, tile_rows(weights, shift), 0.0
    ).astype(BF16)


def gather_kernel(
    x_ref,
    pair_ref,
    present_ref,
    amino_ref,
    offset_ref,
    blocks_ref,
    biases_ref,
    lines,
    offsets,
    send_sem,
    recv_sem,
    bias_send,
    bias_recv,
):
    seq, res = lax.axis_index("seq"), lax.axis_index("res")
    core, y, z = res % 2, (res // 2) % 4, res // 8
    up, down, across = (y + 1) % 4, (y + 3) % 4, (y + 2) % 4

    def place(z_at, y_at, core_at):
        return (z_at * 4 + y_at) * 2 + core_at

    seq_peers = [seq // 2 * 2 + (1 - seq % 2)] + [(seq + 2 * d) % 8 for d in (1, 2, 3)]
    res_peers = [place((z + d) % 4, y, core) for d in (1, 2, 3)]
    res_peers += [place(z, up, core), place(z, down, core), place(z, y, 1 - core)]
    barrier = pltpu.get_barrier_semaphore()
    for peer in seq_peers:
        pl.semaphore_signal(barrier, inc=1, device_id=(peer, res), device_id_type=MESH)
    for peer in res_peers:
        pl.semaphore_signal(barrier, inc=1, device_id=(seq, peer), device_id_type=MESH)

    for tile in range(PAIRS):
        lines[:, tile, :] = x_ref[:, tile * LANES : (tile + 1) * LANES].astype(F32)
    values = lines[...].reshape(SEQS * PAIRS, LANES).astype(BF16)
    blocks_ref[res, PAIRS:ROWS, :] = normalize(values, 64).astype(BF16)
    kept = (present_ref[...] * amino_ref[...]).astype(F32).astype(BF16)
    turned = jnp.zeros((PAIRS, LANES), F32)
    for parity in range(2):
        shape = (PAIRS, SEQS)
        picked = dot_nt(flag(lanes_of(shape) == 2 * rows_of(shape) + parity), kept)
        shape = (SEQS, LANES)
        turned += dot(
            picked.astype(BF16), flag(lanes_of(shape) == rows_of(shape) + parity * SEQS)
        )
    blocks_ref[res, 0:PAIRS, :] = jnp.where(
        lanes_of((PAIRS, LANES)) < 64, 1000000000.0 * (turned - 1.0), 1.0
    ).astype(BF16)

    pl.semaphore_wait(barrier, len(seq_peers) + len(res_peers))

    def chunk(block, group):
        start, size = SPANS[group]
        return blocks_ref.at[block, pl.ds(start, size), :]

    def copy(block, group, slot, target):
        return pltpu.make_async_remote_copy(
            src_ref=chunk(block, group),
            dst_ref=chunk(block, group),
            send_sem=send_sem.at[group, slot],
            recv_sem=recv_sem.at[block, group],
            device_id=(seq, target),
            device_id_type=MESH,
        )

    def arrived(block, group):
        copy(block, group, 0, res).wait_recv()

    sent = []

    def send(block, group, slot, target):
        copy(block, group, slot, target).start()

    for group in range(GROUPS):
        for d in (1, 2, 3):
            send(res, group, d - 1, res_peers[d - 1])

    shape = (8, 8)
    offset_turned = dot_nt(flag(rows_of(shape) == lanes_of(shape)), offset_ref[...]).astype(BF16)

    def bias_rows(step, carry):
        pair = pair_ref[pl.ds(step * 4, 4)].reshape(4 * LANES, LANES)
        normed = normalize(pair, LANES).astype(BF16)
        found = dot_nt(offset_turned, normed)
        for row in range(4):
            offsets[pl.ds(pl.multiple_of(step * 32 + row * 8, 8), 8), :] = found[
                :, row * LANES : (row + 1) * LANES
            ]
        return carry

    lax.fori_loop(0, 8, bias_rows, 0)
    for head in range(8):
        for parity in range(2):
            biases_ref[seq, pl.ds(head * 32 + parity * 16, 16), :] = offsets[
                pl.ds(parity * 8 + head, 16, stride=16), :
            ].astype(BF16)

    def bias_copy(block, slot, target):
        return pltpu.make_async_remote_copy(
            src_ref=biases_ref.at[block],
            dst_ref=biases_ref.at[block],
            send_sem=bias_send.at[slot],
            recv_sem=bias_recv.at[block],
            device_id=(target, res),
            device_id_type=MESH,
        )

    for slot, peer in enumerate(seq_peers):
        bias_copy(seq, slot, peer).start()

    def stage_near(group):
        for at in range(4):
            block = place(at, y, core)

            @pl.when(z != at)
            def _():
                arrived(block, group)

            send(block, group, 3 + at, res_peers[3])
            send(block, group, 7 + at, res_peers[4])
            send(block, group, 11 + at, res_peers[5])

    def stage_next(group):
        for at in range(4):
            low, high = place(at, down, core), place(at, up, core)
            arrived(low, group)
            if at % 2 == 0:
                send(low, group, 15 + at, res_peers[3])
            send(low, group, 19 + at, res_peers[5])
            arrived(high, group)
            if at % 2 == 1:
                send(high, group, 15 + at, res_peers[4])
            send(high, group, 23 + at, res_peers[5])

    def stage_far(group):
        for at in range(4):
            far = place(at, across, core)
            arrived(far, group)
            send(far, group, 27 + at, res_peers[5])

    def stage_core(group):
        for at in range(4):
            for row in range(4):
                arrived(place(at, row, 1 - core), group)

    partner = seq_peers[0]
    for step in range(GROUPS + 3):
        if step < GROUPS:
            stage_near(step)
        if step == 0:
            bias_copy(partner, 0, seq).wait_recv()
            for slot, peer in enumerate(seq_peers[1:]):
                bias_copy(partner, 4 + slot, peer).start()
        if 0 <= step - 1 < GROUPS:
            stage_next(step - 1)
        if 0 <= step - 2 < GROUPS:
            stage_far(step - 2)
        if 0 <= step - 3 < GROUPS:
            stage_core(step - 3)
    for peer in seq_peers[1:]:
        bias_copy(peer, 0, seq).wait_recv()
        bias_copy(peer // 2 * 2 + (1 - peer % 2), 0, seq).wait_recv()
    for slot in range(7):
        bias_copy(seq, slot, seq).wait_send()
    for group in range(GROUPS):
        for slot in range(31):
            copy(res, group, slot, res).wait_send()


def attend_kernel(
    blocks_ref, biases_ref, weights_ref, gated_ref, bias, queries, gates
):
    res = lax.axis_index("res")
    own = blocks_ref[res, PAIRS:ROWS, :]
    weights = weights_ref[...]
    square = (LANES, LANES)
    row, lane = rows_of(square), lanes_of(square)

    wide = (LANES, 256)
    turned = dot_nt(flag(lanes_of(wide) == rows_of(wide) % 64 + 64), weights).astype(BF16)
    across = (64, LANES)
    turned = dot(turned, flag(rows_of(across) == lanes_of(across) % 64))
    query_weights = tile_rows(weights, 0)
    gate_weights = tile_rows(weights, 192)
    for side in range(2):
        mine = row // 64 == side
        query = dot(own, jnp.where(mine, query_weights, 0.0).astype(BF16))
        query = (query * (LOG2E * 8**-0.5)).astype(BF16)
        gate = dot(own, jnp.where(mine, gate_weights, 0.0).astype(BF16))
        gates[:, side * 16 : side * 16 + 16, :] = jax.nn.sigmoid(gate).reshape(
            SEQS, PAIRS, LANES
        )
        for head in range(8):
            keyed = jnp.where(row // 8 == head, turned, 0.0)
            both = jnp.concatenate(
                [jnp.where(lane // 64 == parity, keyed, 0.0) for parity in range(2)], axis=1
            ).astype(BF16)
            found = dot(query, both).astype(BF16)
            for parity in range(2):
                start = (parity * 8 + head) * 32 + side * 16
                queries[:, start : start + 16, :] = found[
                    :, parity * LANES : (parity + 1) * LANES
                ].reshape(SEQS, PAIRS, LANES)

    shape = (256, 256)
    order = flag(rows_of(shape) == 2 * (lanes_of(shape) % LANES) + lanes_of(shape) // LANES)
    for tile in range(4):
        both = jnp.concatenate([biases_ref[2 * tile], biases_ref[2 * tile + 1]], axis=1)
        placed = dot(both, order) * LOG2E
        for parity in range(2):
            bias[parity * 256 : parity * 256 + 256, tile * LANES : (tile + 1) * LANES] = placed[
                :, parity * LANES : (parity + 1) * LANES
            ]

    value_weights = jnp.where(lane >= 64, tile_rows(weights, 128), 0.0).astype(BF16)
    mask = blocks_ref[:, 0:PAIRS, :].reshape(512, LANES)
    half = lanes_of((256, LANES)) < 64
    head_of = lanes_of((32, LANES)) // 8 - 8

    def one_line(line, carry):
        start = pl.multiple_of(PAIRS + line * PAIRS, PAIRS)
        keys = blocks_ref[:, pl.ds(start, PAIRS), :].reshape(512, LANES)
        right = jnp.concatenate([keys, mask], axis=1)
        tall = (512, LANES)
        picks = flag(lanes_of(tall) == rows_of(tall) // 256 * SEQS + line)
        left = jnp.concatenate([queries[line], picks], axis=1)
        logits = dot_nt(left, right) + bias[...]
        peak = jnp.max(logits, axis=1, keepdims=True)
        peak = jnp.maximum(peak[:256], peak[256:])
        exped = jnp.exp2(logits - jnp.concatenate([peak, peak], axis=0)).astype(BF16)
        summed = dot(exped, right)
        taken = jnp.where(half, summed[:256, :LANES], summed[256:, :LANES]).astype(BF16)
        total = summed[:256, LANES:] + summed[256:, LANES:]
        found = dot(taken, value_weights) / total
        attended = jnp.zeros((32, LANES), F32)
        for head in range(8):
            attended = jnp.where(head_of == head, found[head * 32 : head * 32 + 32], attended)
        gated_ref[line] = (gates[line] * attended).astype(BF16)
        return carry

    lax.fori_loop(0, SEQS, one_line, 0)


def column_kernel(
    x_ref,
    gated_ref,
    present_ref,
    amino_ref,
    exit_ref,
    weights_ref,
    exit_col_ref,
    out_ref,
    lines,
    results,
    means,
    sums,
    mean_send,
    mean_recv,
    sum_send,
    sum_recv,
):
    seq, res = lax.axis_index("seq"), lax.axis_index("res")
    peers = [(seq + d) % 8 for d in range(1, 8)]
    barrier = pltpu.get_barrier_semaphore()
    for peer in peers:
        pl.semaphore_signal(barrier, inc=1, device_id=(peer, res), device_id_type=MESH)

    for tile in range(PAIRS):
        lines[:, tile, :] = x_ref[:, tile * LANES : (tile + 1) * LANES].astype(F32)
    spread = (RES, RES * 64)
    kept = (present_ref[...] * amino_ref[...]).astype(F32).astype(BF16)
    kept = dot(kept, flag(rows_of(spread) == lanes_of(spread) // 64))
    for tile in range(PAIRS):
        results[:, tile, :] = kept[:, tile * LANES : (tile + 1) * LANES]
    kept = results[...]

    square = (LANES, LANES)
    row, lane = rows_of(square), lanes_of(square)
    exits = tile_rows(exit_ref[...], 0)
    update = jnp.zeros((SEQS * PAIRS, LANES), F32)
    for side in range(2):
        exit_side = jnp.where((row >= 64) & (lane // 64 == side), exits, 0.0).astype(BF16)
        gated = gated_ref[:, side * 16 : side * 16 + 16, :].reshape(SEQS * PAIRS, LANES)
        update += dot(gated, exit_side)
    whole = (SEQS, PAIRS, LANES)
    flat = (SEQS * PAIRS, LANES)
    line = (lines[...].reshape(flat) + update).astype(BF16)
    normed = normalize(line, 64).astype(BF16)

    pl.semaphore_wait(barrier, 7)

    def exchange(buffer, send_sem, recv_sem):
        def copy(source, slot, target):
            return pltpu.make_async_remote_copy(
                src_ref=buffer.at[source],
                dst_ref=buffer.at[source],
                send_sem=send_sem.at[slot],
                recv_sem=recv_sem.at[source],
                device_id=(target, res),
                device_id_type=MESH,
            )

        for slot, peer in enumerate(peers):
            copy(seq, slot, peer).start()
        return copy

    means[seq, 0:16, :] = jnp.sum(kept * normed.astype(F32).reshape(whole), axis=0)
    means[seq, 16:32, :] = jnp.sum(kept, axis=0)
    mean_copy = exchange(means, mean_send, mean_recv)

    weights = weights_ref[...]
    gate = jax.nn.sigmoid(dot(normed, twice(weights, 64)))
    width = weights.shape[1]
    pick_shape = (width, LANES)
    column, at = rows_of(pick_shape), lanes_of(pick_shape)
    tall = dot(flag(row[:, :64] % 64 == lane[:, :64]), weights).astype(BF16)
    same = row // 64 == lane // 64
    key_weights = jnp.where(same, dot(tall, flag(column == 128 + at % 8)), 0.0).astype(BF16)
    value_weights = jnp.where(same, dot(tall, flag(column == 136 + at % 8)), 0.0).astype(BF16)
    query_weights = twice(weights, 0)
    key = dot(normed, key_weights).reshape(whole)
    value = dot(normed, value_weights).reshape(whole)
    head_sum = flag(row // 8 == lane // 8)

    for slot, peer in enumerate(peers):
        mean_copy(peer, slot, seq).wait_recv()
    total = jnp.sum(means[...], axis=0)
    mean = total[:16] / jnp.maximum(total[16:], 1.0)
    mean_query = dot_split(mean, query_weights) * 8**-0.5
    logits = dot_split((key * mean_query[None]).reshape(flat), head_sum).reshape(whole)
    logits = logits + 1000000000.0 * (kept - 1.0)
    peak = jnp.max(logits, axis=0)
    exped = jnp.exp(logits - peak[None])
    sums[seq, 0:16, :] = peak
    sums[seq, 16:32, :] = jnp.sum(exped, axis=0)
    sums[seq, 32:48, :] = jnp.sum(exped * value, axis=0)
    sum_copy = exchange(sums, sum_send, sum_recv)
    for slot, peer in enumerate(peers):
        sum_copy(peer, slot, seq).wait_recv()
    peaks = sums[:, 0:16, :]
    factor = jnp.exp(peaks - jnp.max(peaks, axis=0)[None])
    attended = jnp.sum(factor * sums[:, 32:48, :], axis=0) / jnp.sum(
        factor * sums[:, 16:32, :], axis=0
    )
    gated = (gate.reshape(whole) * attended[None]).astype(BF16).reshape(flat)
    final = line.astype(F32) + dot(gated, twice(exit_col_ref[...], 0))
    results[...] = final.reshape(whole)
    for tile in range(PAIRS):
        out_ref[:, tile * LANES : (tile + 1) * LANES] = results[:, tile, :].astype(BF16)
    for slot in range(7):
        mean_copy(seq, slot, seq).wait_send()
        sum_copy(seq, slot, seq).wait_send()


def on_device(
    extra_activations,
    twofold_representation,
    present_indicator,
    amino_presence,
    twofold_offset_matrix,
    horizontal_matrix,
    horizontal_exit_matrix,
    vertical_matrix,
    vertical_exit_matrix,
):
    vmem = pl.BlockSpec(memory_space=pltpu.VMEM)
    amino_row = amino_presence.reshape(1, RES)
    blocks, biases = pl.pallas_call(
        gather_kernel,
        out_shape=(
            jax.ShapeDtypeStruct((RES, ROWS, LANES), BF16),
            jax.ShapeDtypeStruct((8, 256, LANES), BF16),
        ),
        in_specs=[vmem] * 5,
        out_specs=(vmem, vmem),
        scratch_shapes=[
            pltpu.VMEM((SEQS, PAIRS, LANES), F32),
            pltpu.VMEM((256, LANES), F32),
            pltpu.SemaphoreType.DMA((GROUPS, 31)),
            pltpu.SemaphoreType.DMA((RES, GROUPS)),
            pltpu.SemaphoreType.DMA((7,)),
            pltpu.SemaphoreType.DMA((8,)),
        ],
        compiler_params=pltpu.CompilerParams(
            collective_id=0, has_side_effects=True, vmem_limit_bytes=32 << 20
        ),
        name="gather",
    )(
        extra_activations,
        twofold_representation,
        present_indicator,
        amino_row,
        twofold_offset_matrix,
    )
    gated = pl.pallas_call(
        attend_kernel,
        out_shape=jax.ShapeDtypeStruct((SEQS, 32, LANES), BF16),
        in_specs=[vmem] * 3,
        out_specs=vmem,
        scratch_shapes=[
            pltpu.VMEM((512, 512), F32),
            pltpu.VMEM((SEQS, 512, LANES), BF16),
            pltpu.VMEM((SEQS, 32, LANES), F32),
        ],
        compiler_params=pltpu.CompilerParams(vmem_limit_bytes=40 << 20),
        name="attend",
    )(blocks, biases, horizontal_matrix)
    return pl.pallas_call(
        column_kernel,
        out_shape=jax.ShapeDtypeStruct((SEQS, RES * 64), BF16),
        in_specs=[vmem] * 7,
        out_specs=vmem,
        scratch_shapes=[
            pltpu.VMEM((SEQS, PAIRS, LANES), F32),
            pltpu.VMEM((SEQS, PAIRS, LANES), F32),
            pltpu.VMEM((8, 32, LANES), F32),
            pltpu.VMEM((8, 48, LANES), F32),
            pltpu.SemaphoreType.DMA((7,)),
            pltpu.SemaphoreType.DMA((8,)),
            pltpu.SemaphoreType.DMA((7,)),
            pltpu.SemaphoreType.DMA((8,)),
        ],
        compiler_params=pltpu.CompilerParams(
            collective_id=1, has_side_effects=True, vmem_limit_bytes=32 << 20
        ),
        name="column",
    )(
        extra_activations,
        gated,
        present_indicator,
        amino_row,
        horizontal_exit_matrix,
        vertical_matrix,
        vertical_exit_matrix,
    )


def solution(mesh):
    in_specs = (
        P("seq", "res"),
        P("res", "seq", None),
        P("seq", "res"),
        P("res"),
        P(),
        P(),
        P(),
        P(),
        P(),
    )
    out_specs = P("seq", "res")
    return jax.shard_map(
        on_device, mesh=mesh, in_specs=in_specs, out_specs=out_specs, check_vma=False
    )
```

time: 309 us -> 102 us (0.33)
  the two profiles are of different devices: /device:TPU:32 before, /device:TPU:24 now
where the time goes in v1:
time: 102 us
  Pallas kernels  95.9 us (94%)
  local copies, waits for them, and re-layouts  5.77 us (6%)
    pallas_call x1, Pallas kernels, on_device(): pl.pallas_call(gather_kernel, out_shape=(jax.ShapeDtypeStruct((RES, ROWS,...  42.9 us
    pallas_call x1, Pallas kernels, on_device(): pl.pallas_call(attend_kernel, out_shape=jax.ShapeDtypeStruct((SEQS, 32, L...  33.1 us
    pallas_call x1, Pallas kernels, on_device(): pl.pallas_call(column_kernel, out_shape=jax.ShapeDtypeStruct((SEQS, RES *...  19.9 us
    unnamed x24, local copies, waits for them, and re-layouts  5.77 us

profile of v1, /device:TPU:24, one launch (start us, length us, event | category | flops | bytes accessed | tf_op | source)
XLA Modules:
  0.0 101.8 jit_solution(17606187287206873568)
XLA Ops:
  0.0 0.0 copy-start.4
  0.0 0.0 copy-start.7
  0.0 0.0 copy-start.10
  0.0 0.8 copy.10.offset_ref
  0.8 0.0 copy-start
  0.8 1.2 %copy-done = bf16[32,128,128]{2,1,0:T(8,128)(2,1)S(1)} copy-done((bf16[32,128,128]{2,1,0:T(8,128)(2,1)S(1)}, bf16[32,128,128]{2,1,0:T(8,128)(2,1)}, u32[]{:S(2)}) %copy-start) | copy-done | bytes 1048600
  2.1 0.0 copy-start.1
  2.1 0.9 copy-done.1
  3.0 0.0 copy-start.3
  3.0 0.7 copy-done.3
  3.7 0.0 copy-start.9
  3.7 0.7 copy-done.9
  4.4 0.0 copy-start.2
  4.4 0.0 copy-start.6
  4.4 0.0 copy-start.8
  4.4 42.9 %gather.1 = (bf16[32,528,128]{2,1,0:T(8,128)(2,1)S(1)}, bf16[8,256,128]{2,1,0:T(8,128)(2,1)S(1)}) custom-call(bf16[32,2048]{1,0:T(8,128)(2,1)S(1)} %copy-done.1, bf16[32,128,128]{2,1,0:T(8,128)(2,1)S(1)} %copy-done, s32[32,32]{1,0:T(8,128)S(1)} %copy-done.3, s32[1,32]{1,0:T(1,128)S(1)} %bitcast.1, bf16[128,8]{1,0:T(8,128)(2,1)S(1)} %copy.10.offset_ref), custom_call_target="tpu_custom_call" | custom-call | tf_op jit(solution)/shard_map/gather/pallas_call | solution.py:436
  47.3 0.0 copy-start.5
  47.3 0.7 copy-done.5
  48.0 33.1 %attend.1.gated_ref = bf16[32,32,128]{2,1,0:T(8,128)(2,1)S(1)} custom-call(bf16[32,528,128]{2,1,0:T(8,128)(2,1)S(1)} %get-tuple-element.7.blocks_ref, bf16[8,256,128]{2,1,0:T(8,128)(2,1)S(1)} %get-tuple-element.8.biases_ref, bf16[64,256]{1,0:T(8,128)(2,1)S(1)} %copy-done.5), custom_call_target="tpu_custom_call" | custom-call | tf_op jit(solution)/shard_map/attend/pallas_call | solution.py:463
  81.2 0.0 copy-done.4
  81.2 0.0 copy-done.7
  81.2 0.0 copy-done.10
  81.2 0.0 copy-done.2
  81.2 0.0 copy-done.6
  81.2 0.0 copy-done.8
  81.2 19.9 %column.1 = bf16[32,2048]{1,0:T(8,128)(2,1)S(1)} custom-call(bf16[32,2048]{1,0:T(8,128)(2,1)S(1)} %copy-done.2, bf16[32,32,128]{2,1,0:T(8,128)(2,1)S(1)} %attend.1.gated_ref, s32[32,32]{1,0:T(8,128)S(1)} %copy-done.4, s32[1,32]{1,0:T(1,128)S(1)} %bitcast.2, bf16[64,64]{1,0:T(8,128)(2,1)S(1)} %copy-done.7, bf16[64,144]{1,0:T(8,128)(2,1)S(1)} %copy-done.6, ...), custom_call_target="tpu_custom_call" | custom-call | tf_op jit(solution)/shard_map/column/pallas_call | solution.py:476
  101.1 0.7 copy.12
Async XLA Ops:
  0.0 81.2 %copy-start.4 = (s32[32,32]{1,0:T(8,128)S(1)}, s32[32,32]{1,0:T(8,128)}, u32[]{:S(2)}) copy-start(s32[32,32]{1,0:T(8,128)} %present_ref.3) | copy-start | bytes 12292
  0.0 81.2 %copy-start.7 = (bf16[64,64]{1,0:T(8,128)(2,1)S(1)}, bf16[64,64]{1,0:T(8,128)(2,1)}, u32[]{:S(2)}) copy-start(bf16[64,64]{1,0:T(8,128)(2,1)} %exit_ref.1) | copy-start | bytes 24580
  0.0 81.2 %copy-start.10 = (s32[32]{0:T(128)S(1)}, s32[32]{0:T(128)}, u32[]{:S(2)}) copy-start(s32[32]{0:T(128)} %param.12) | copy-start | bytes 388
  0.8 1.2 %copy-start = (bf16[32,128,128]{2,1,0:T(8,128)(2,1)S(1)}, bf16[32,128,128]{2,1,0:T(8,128)(2,1)}, u32[]{:S(2)}) copy-start(bf16[32,128,128]{2,1,0:T(8,128)(2,1)} %pair_ref.1) | copy-start | bytes 3145732
  2.1 0.9 copy-start.1
  3.0 0.7 copy-start.3
  3.7 0.7 copy-start.9
  4.4 76.8 %copy-start.2 = (bf16[32,2048]{1,0:T(8,128)(2,1)S(1)}, bf16[32,2048]{1,0:T(8,128)(2,1)}, u32[]{:S(2)}) copy-start(bf16[32,2048]{1,0:T(8,128)(2,1)} %x_ref.3) | copy-start | bytes 393220
  4.4 76.8 %copy-start.6 = (bf16[64,144]{1,0:T(8,128)(2,1)S(1)}, bf16[64,144]{1,0:T(8,128)(2,1)}, u32[]{:S(2)}) copy-start(bf16[64,144]{1,0:T(8,128)(2,1)} %weights_ref.3) | copy-start | bytes 55300
  4.4 76.9 %copy-start.8 = (bf16[64,64]{1,0:T(8,128)(2,1)S(1)}, bf16[64,64]{1,0:T(8,128)(2,1)}, u32[]{:S(2)}) copy-start(bf16[64,64]{1,0:T(8,128)(2,1)} %exit_col_ref.1) | copy-start | bytes 24580
  47.3 0.8 copy-start.5

commit v2 on v1

v2 whole, which is shorter than its diff:
```python
import jax
import jax.numpy as jnp
from jax import lax
from jax.experimental import pallas as pl
from jax.experimental.pallas import tpu as pltpu
from jax.sharding import PartitionSpec as P

MESH = pl.DeviceIdType.MESH
F32, BF16 = jnp.float32, jnp.bfloat16
SEQS, RES, PAIRS, LANES = 32, 32, 16, 128
ROWS = PAIRS + SEQS * PAIRS
GROUPS = 4
PER_GROUP = SEQS // GROUPS
LOG2E = 1.4426950408889634
SPANS = [
    (0 if g == 0 else PAIRS + g * PER_GROUP * PAIRS, PER_GROUP * PAIRS + (PAIRS if g == 0 else 0)) for g in range(GROUPS)
]


def rows_of(shape):
    return lax.broadcasted_iota(jnp.int32, shape, 0)


def lanes_of(shape):
    return lax.broadcasted_iota(jnp.int32, shape, 1)


def flag(condition):
    return jnp.where(condition, 1.0, 0.0).astype(BF16)


def dot(left, right):
    return jnp.dot(left, right, preferred_element_type=F32)


def dot_nt(left, right):
    return lax.dot_general(left, right, (((1,), (1,)), ((), ())), preferred_element_type=F32)


def dot_split(left, right):
    high = left.astype(BF16)
    low = (left - high.astype(F32)).astype(BF16)
    return dot(high, right) + dot(low, right)


def normalize(values, width, coarse=False):
    shape = (LANES, LANES)
    average = jnp.where(
        rows_of(shape) // width == lanes_of(shape) // width, 1.0 / width, 0.0
    ).astype(BF16)
    centre = values.astype(F32) - dot(values, average)
    squares = centre * centre
    spread = dot(squares.astype(BF16), average) if coarse else dot_split(squares, average)
    return centre * lax.rsqrt(spread + 1e-05)


def tile_rows(weights, shift):
    height, width = weights.shape
    tall = dot(flag(rows_of((LANES, height)) % height == lanes_of((LANES, height))), weights)
    column = rows_of((width, LANES))
    pick = flag(column == lanes_of((width, LANES)) % 64 + shift)
    return dot(tall.astype(BF16), pick)


def twice(weights, shift):
    shape = (LANES, LANES)
    return jnp.where(
        rows_of(shape) // 64 == lanes_of(shape) // 64, tile_rows(weights, shift), 0.0
    ).astype(BF16)


SCHEDULE = [
    (1, "far", 1),
    (1, "next", 2),
    (3, "core", 1),
    (4, "far", 2),
    (4, "next", 3),
    (7, "core", 2),
    (7, "far", 3),
    (11, "core", 3),
]


def fused_kernel(
    x_hbm,
    pair_hbm,
    present_hbm,
    amino_hbm,
    offset_hbm,
    weights_hbm,
    exit_hbm,
    column_hbm,
    exit_col_hbm,
    out_ref,
    x_ref,
    pair_ref,
    present_ref,
    amino_ref,
    offset_ref,
    weights_ref,
    exit_ref,
    column_ref,
    exit_col_ref,
    blocks,
    biases,
    lines,
    offsets,
    bias,
    queries,
    gates,
    gateds,
    logits_even,
    logits_odd,
    peak_even,
    peak_odd,
    kepts,
    results,
    means,
    sums,
    load_sem,
    send_sem,
    z_recv,
    y_recv,
    far_recv,
    core_recv,
    bias_send,
    bias_recv,
    mean_send,
    mean_recv,
    sum_send,
    sum_recv,
):
    loads = [
        pltpu.make_async_copy(source, target, load_sem.at[slot])
        for slot, (source, target) in enumerate(
            [
                (pair_hbm, pair_ref),
                (offset_hbm, offset_ref),
                (x_hbm, x_ref),
                (present_hbm, present_ref),
                (amino_hbm, amino_ref),
                (weights_hbm, weights_ref),
                (exit_hbm, exit_ref),
                (column_hbm, column_ref),
                (exit_col_hbm, exit_col_ref),
            ]
        )
    ]
    for load in loads:
        load.start()
    seq, res = lax.axis_index("seq"), lax.axis_index("res")
    core, y, z = res % 2, (res // 2) % 4, res // 8
    up, down, across = (y + 1) % 4, (y + 3) % 4, (y + 2) % 4
    partner = seq // 2 * 2 + (1 - seq % 2)
    bias_peers = [partner] + [(seq + 2 * d) % 8 for d in (1, 2, 3)]
    seq_peers = [(seq + d) % 8 for d in range(1, 8)]

    def place(z_at, y_at, core_at):
        return (z_at * 4 + y_at) * 2 + core_at

    z_peers = [place((z + d) % 4, y, core) for d in (1, 2, 3)]
    up_peer, down_peer, core_peer = place(z, up, core), place(z, down, core), place(z, y, 1 - core)
    res_peers = z_peers + [up_peer, down_peer, core_peer]
    barrier = pltpu.get_barrier_semaphore()
    for peer in seq_peers:
        pl.semaphore_signal(barrier, inc=1, device_id=(peer, res), device_id_type=MESH)
    for peer in res_peers:
        pl.semaphore_signal(barrier, inc=1, device_id=(seq, peer), device_id_type=MESH)

    loads[0].wait()
    loads[1].wait()

    def bias_rows(step, carry):
        pair = pair_ref[pl.ds(step * 4, 4)].reshape(4 * LANES, LANES)
        normed = normalize(pair, LANES, coarse=True).astype(BF16)
        found = dot_nt(offset_ref[...], normed)
        for row in range(4):
            offsets[pl.ds(pl.multiple_of(step * 32 + row * 8, 8), 8), :] = found[
                :, row * LANES : (row + 1) * LANES
            ]
        return carry

    lax.fori_loop(0, 8, bias_rows, 0, unroll=2)
    for head in range(8):
        for parity in range(2):
            biases[seq, pl.ds(head * 32 + parity * 16, 16), :] = offsets[
                pl.ds(parity * 8 + head, 16, stride=16), :
            ].astype(BF16)

    whole = (SEQS, PAIRS, LANES)
    flat = (SEQS * PAIRS, LANES)
    for load in loads[2:5]:
        load.wait()
    for tile in range(PAIRS):
        lines[:, tile, :] = x_ref[:, tile * LANES : (tile + 1) * LANES].astype(F32)
    own = normalize(lines[...].reshape(flat).astype(BF16), 64).astype(BF16)
    blocks[z, y, core, PAIRS:ROWS, :] = own
    kept = (present_ref[...] * amino_ref[...]).astype(F32).astype(BF16)
    turned = jnp.zeros((PAIRS, LANES), F32)
    for parity in range(2):
        shape = (PAIRS, SEQS)
        picked = dot_nt(flag(lanes_of(shape) == 2 * rows_of(shape) + parity), kept)
        shape = (SEQS, LANES)
        turned += dot(
            picked.astype(BF16), flag(lanes_of(shape) == rows_of(shape) + parity * SEQS)
        )
    blocks[z, y, core, 0:PAIRS, :] = jnp.where(
        lanes_of((PAIRS, LANES)) < 64, 1000000000.0 * (turned - 1.0), 1.0
    ).astype(BF16)

    def remote(view, send, recv, target):
        return pltpu.make_async_remote_copy(
            src_ref=view,
            dst_ref=view,
            send_sem=send,
            recv_sem=recv,
            device_id=(seq, target),
            device_id_type=MESH,
        )

    def one(z_at, group):
        return blocks.at[z_at, y, core, pl.ds(*SPANS[group]), :]

    def column(y_at, core_at, group, first=0, count=4):
        return blocks.at[pl.ds(first, count), y_at, core_at, pl.ds(*SPANS[group]), :]

    def z_copy(group, d):
        return remote(one(z, group), send_sem.at[group, d - 1], z_recv.at[z, group], z_peers[d - 1])

    def z_wait(group, d):
        at = (z + d) % 4
        remote(one(at, group), send_sem.at[group, 0], z_recv.at[at, group], res).wait_recv()

    def y_copy(group, side, source):
        target = (up_peer, down_peer)[side]
        return remote(
            column(source, core, group),
            send_sem.at[group, 3 + side],
            y_recv.at[1 - side, group],
            target,
        )

    def far_copy(group, side, source):
        target = (up_peer, down_peer)[side]
        return remote(
            column(source, core, group, 2 * side, 2),
            send_sem.at[group, 5 + side],
            far_recv.at[side, group],
            target,
        )

    def core_copy(group, slot, source, core_at):
        return remote(
            column(source, core_at, group),
            send_sem.at[group, 7 + slot],
            core_recv.at[source, group],
            core_peer,
        )

    def stage_near(group):
        for d in (1, 2, 3):
            z_wait(group, d)
        y_copy(group, 0, y).start()
        y_copy(group, 1, y).start()
        core_copy(group, 0, y, core).start()

    def stage_next(group):
        y_copy(group, 0, down).wait_recv()
        far_copy(group, 0, down).start()
        core_copy(group, 1, down, core).start()
        y_copy(group, 1, up).wait_recv()
        far_copy(group, 1, up).start()
        core_copy(group, 2, up, core).start()

    def stage_far(group):
        far_copy(group, 0, across).wait_recv()
        far_copy(group, 1, across).wait_recv()
        core_copy(group, 3, across, core).start()

    def stage_core(group):
        for at in range(4):
            core_copy(group, 0, at, 1 - core).wait_recv()

    def bias_copy(block, slot, target):
        return pltpu.make_async_remote_copy(
            src_ref=biases.at[block],
            dst_ref=biases.at[block],
            send_sem=bias_send.at[slot],
            recv_sem=bias_recv.at[block],
            device_id=(target, res),
            device_id_type=MESH,
        )

    pl.semaphore_wait(barrier, len(seq_peers) + len(res_peers))
    for d in (1, 2, 3):
        z_copy(0, d).start()
    for slot, peer in enumerate(bias_peers):
        bias_copy(seq, slot, peer).start()
    for group in range(1, GROUPS):
        for d in (1, 2, 3):
            z_copy(group, d).start()

    for load in loads[5:]:
        load.wait()
    weights = weights_ref[...]
    square = (LANES, LANES)
    row, lane = rows_of(square), lanes_of(square)
    wide = (LANES, 256)
    turned = dot_nt(flag(lanes_of(wide) == rows_of(wide) % 64 + 64), weights).astype(BF16)
    shape = (64, LANES)
    turned = dot(turned, flag(rows_of(shape) == lanes_of(shape) % 64))
    query_weights = tile_rows(weights, 0)
    gate_weights = tile_rows(weights, 192)

    def query_side(side):
        mine = row // 64 == side
        query = dot(own, jnp.where(mine, query_weights, 0.0).astype(BF16))
        query = (query * (LOG2E * 8**-0.5)).astype(BF16)
        gate = dot(own, jnp.where(mine, gate_weights, 0.0).astype(BF16))
        gates[:, side * 16 : side * 16 + 16, :] = jax.nn.sigmoid(gate).reshape(whole)
        for head in range(8):
            keyed = jnp.where(row // 8 == head, turned, 0.0)
            both = jnp.concatenate(
                [jnp.where(lane // 64 == parity, keyed, 0.0) for parity in range(2)], axis=1
            ).astype(BF16)
            found = dot(query, both).astype(BF16)
            for parity in range(2):
                start = (parity * 8 + head) * 32 + side * 16
                queries[:, start : start + 16, :] = found[
                    :, parity * LANES : (parity + 1) * LANES
                ].reshape(whole)

    query_side(0)
    stage_near(0)
    query_side(1)
    stage_near(1)
    bias_copy(partner, 0, seq).wait_recv()
    for slot, peer in enumerate(bias_peers[1:]):
        bias_copy(partner, 4 + slot, peer).start()

    spread = (RES, RES * 64)
    kept = dot(kept, flag(rows_of(spread) == lanes_of(spread) // 64))
    for tile in range(PAIRS):
        kepts[:, tile, :] = kept[:, tile * LANES : (tile + 1) * LANES]

    stage_next(0)
    stage_near(2)
    stage_far(0)
    stage_near(3)
    stage_next(1)
    for peer in bias_peers[1:]:
        bias_copy(peer, 0, seq).wait_recv()
        bias_copy(peer // 2 * 2 + (1 - peer % 2), 0, seq).wait_recv()
    shape = (256, 256)
    order = flag(rows_of(shape) == 2 * (lanes_of(shape) % LANES) + lanes_of(shape) // LANES)
    for tile in range(4):
        both = jnp.concatenate([biases[2 * tile], biases[2 * tile + 1]], axis=1)
        placed = dot(both, order) * LOG2E
        for parity in range(2):
            bias[parity * 256 : parity * 256 + 256, tile * LANES : (tile + 1) * LANES] = placed[
                :, parity * LANES : (parity + 1) * LANES
            ]
    stage_core(0)

    value_weights = jnp.where(lane >= 64, tile_rows(weights, 128), 0.0).astype(BF16)
    half = lanes_of((256, LANES)) < 64
    head_of = lanes_of((32, LANES)) // 8 - 8

    def keys_of(line):
        start = pl.multiple_of(PAIRS + line * PAIRS, PAIRS)
        keys = blocks[:, :, :, pl.ds(start, PAIRS), :].reshape(512, LANES)
        mask = blocks[:, :, :, 0:PAIRS, :].reshape(512, LANES)
        return jnp.concatenate([keys, mask], axis=1)

    def score(line, logits_ref, peak_ref):
        at = lanes_of((PAIRS, LANES))
        picks = [flag(at == line)] * 16 + [flag(at == line + SEQS)] * 16
        left = jnp.concatenate([queries[line], jnp.concatenate(picks, axis=0)], axis=1)
        logits = dot_nt(left, keys_of(line)) + bias[...]
        logits_ref[...] = logits
        peak = jnp.maximum(
            jnp.maximum(logits[:, 0:128], logits[:, 128:256]),
            jnp.maximum(logits[:, 256:384], logits[:, 384:512]),
        )
        peak = jnp.max(jnp.maximum(peak[:256], peak[256:]), axis=1, keepdims=True)
        peak_ref[...] = jnp.broadcast_to(peak, (256, LANES))

    def weigh(line, logits_ref, peak_ref):
        peak = jnp.concatenate([peak_ref[...]] * 4, axis=1)
        peak = jnp.concatenate([peak, peak], axis=0)
        exped = jnp.exp2(logits_ref[...] - peak).astype(BF16)
        summed = dot(exped, keys_of(line))
        taken = jnp.where(half, summed[:256, :LANES], summed[256:, :LANES]).astype(BF16)
        total = summed[:256, LANES:] + summed[256:, LANES:]
        found = dot(taken, value_weights) / total
        attended = jnp.zeros((32, LANES), F32)
        for head in range(8):
            attended = jnp.where(head_of == head, found[head * 32 : head * 32 + 32], attended)
        gateds[line] = (gates[line] * attended).astype(BF16)

    score(0, logits_even, peak_even)

    def two_lines(step, carry):
        for at, stage, group in SCHEDULE:

            @pl.when(step == at)
            def _():
                {"next": stage_next, "far": stage_far, "core": stage_core}[stage](group)

        line = 2 * step
        score(line + 1, logits_odd, peak_odd)
        weigh(line, logits_even, peak_even)
        score(jnp.minimum(line + 2, SEQS - 1), logits_even, peak_even)
        weigh(line + 1, logits_odd, peak_odd)
        return carry

    lax.fori_loop(0, SEQS // 2, two_lines, 0)

    exits = tile_rows(exit_ref[...], 0)
    update = jnp.zeros(flat, F32)
    for side in range(2):
        exit_side = jnp.where((row >= 64) & (lane // 64 == side), exits, 0.0).astype(BF16)
        update += dot(gateds[:, side * 16 : side * 16 + 16, :].reshape(flat), exit_side)
    line = (lines[...].reshape(flat) + update).astype(BF16)
    normed = normalize(line, 64).astype(BF16)

    def exchange(buffer, send, recv):
        def copy(source, slot, target):
            return pltpu.make_async_remote_copy(
                src_ref=buffer.at[source],
                dst_ref=buffer.at[source],
                send_sem=send.at[slot],
                recv_sem=recv.at[source],
                device_id=(target, res),
                device_id_type=MESH,
            )

        for slot, peer in enumerate(seq_peers):
            copy(seq, slot, peer).start()
        return copy

    kept = kepts[...]
    means[seq, 0:16, :] = jnp.sum(kept * normed.astype(F32).reshape(whole), axis=0)
    means[seq, 16:32, :] = jnp.sum(kept, axis=0)
    mean_copy = exchange(means, mean_send, mean_recv)

    weights = column_ref[...]
    gate = jax.nn.sigmoid(dot(normed, twice(weights, 64)))
    pick_shape = (weights.shape[1], LANES)
    source, at = rows_of(pick_shape), lanes_of(pick_shape)
    tall = dot(flag(row[:, :64] % 64 == lane[:, :64]), weights).astype(BF16)
    same = row // 64 == lane // 64
    key_weights = jnp.where(same, dot(tall, flag(source == 128 + at % 8)), 0.0).astype(BF16)
    value_weights = jnp.where(same, dot(tall, flag(source == 136 + at % 8)), 0.0).astype(BF16)
    query_weights = twice(weights, 0)
    key = dot(normed, key_weights).reshape(whole)
    value = dot(normed, value_weights).reshape(whole)
    head_sum = flag(row // 8 == lane // 8)

    for slot, peer in enumerate(seq_peers):
        mean_copy(peer, slot, seq).wait_recv()
    total = jnp.sum(means[...], axis=0)
    mean = total[:16] / jnp.maximum(total[16:], 1.0)
    mean_query = dot_split(mean, query_weights) * 8**-0.5
    logits = dot_split((key * mean_query[None]).reshape(flat), head_sum).reshape(whole)
    logits = logits + 1000000000.0 * (kept - 1.0)
    peak = jnp.max(logits, axis=0)
    exped = jnp.exp(logits - peak[None])
    sums[seq, 0:16, :] = peak
    sums[seq, 16:32, :] = jnp.sum(exped, axis=0)
    sums[seq, 32:48, :] = jnp.sum(exped * value, axis=0)
    sum_copy = exchange(sums, sum_send, sum_recv)
    for slot, peer in enumerate(seq_peers):
        sum_copy(peer, slot, seq).wait_recv()
    peaks = sums[:, 0:16, :]
    factor = jnp.exp(peaks - jnp.max(peaks, axis=0)[None])
    attended = jnp.sum(factor * sums[:, 32:48, :], axis=0) / jnp.sum(
        factor * sums[:, 16:32, :], axis=0
    )
    gated = (gate.reshape(whole) * attended[None]).astype(BF16).reshape(flat)
    final = line.astype(F32) + dot(gated, twice(exit_col_ref[...], 0))
    results[...] = final.reshape(whole)
    for tile in range(PAIRS):
        out_ref[:, tile * LANES : (tile + 1) * LANES] = results[:, tile, :].astype(BF16)

    for slot in range(7):
        bias_copy(seq, slot, seq).wait_send()
        mean_copy(seq, slot, seq).wait_send()
        sum_copy(seq, slot, seq).wait_send()
    for group in range(GROUPS):
        for d in (1, 2, 3):
            z_copy(group, d).wait_send()
        for side in range(2):
            y_copy(group, side, y).wait_send()
            far_copy(group, side, y).wait_send()
        for slot in range(4):
            core_copy(group, slot, y, core).wait_send()


def on_device(
    extra_activations,
    twofold_representation,
    present_indicator,
    amino_presence,
    twofold_offset_matrix,
    horizontal_matrix,
    horizontal_exit_matrix,
    vertical_matrix,
    vertical_exit_matrix,
):
    operands = [
        extra_activations,
        twofold_representation,
        present_indicator,
        amino_presence.reshape(1, RES),
        twofold_offset_matrix.T,
        horizontal_matrix,
        horizontal_exit_matrix,
        vertical_matrix,
        vertical_exit_matrix,
    ]
    dma, vmem = pltpu.SemaphoreType.DMA, pltpu.VMEM
    return pl.pallas_call(
        fused_kernel,
        out_shape=jax.ShapeDtypeStruct((SEQS, RES * 64), BF16),
        in_specs=[pl.BlockSpec(memory_space=pltpu.HBM)] * len(operands),
        out_specs=pl.BlockSpec(memory_space=vmem),
        scratch_shapes=[vmem(operand.shape, operand.dtype) for operand in operands]
        + [
            vmem((4, 4, 2, ROWS, LANES), BF16),
            vmem((8, 256, LANES), BF16),
            vmem((SEQS, PAIRS, LANES), F32),
            vmem((256, LANES), F32),
            vmem((512, 512), F32),
            vmem((SEQS, 512, LANES), BF16),
            vmem((SEQS, 32, LANES), F32),
            vmem((SEQS, 32, LANES), BF16),
            vmem((512, 512), F32),
            vmem((512, 512), F32),
            vmem((256, LANES), F32),
            vmem((256, LANES), F32),
            vmem((SEQS, PAIRS, LANES), F32),
            vmem((SEQS, PAIRS, LANES), F32),
            vmem((8, 32, LANES), F32),
            vmem((8, 48, LANES), F32),
            dma((len(operands),)),
            dma((GROUPS, 11)),
            dma((4, GROUPS)),
            dma((2, GROUPS)),
            dma((2, GROUPS)),
            dma((4, GROUPS)),
            dma((7,)),
            dma((8,)),
            dma((7,)),
            dma((8,)),
            dma((7,)),
            dma((8,)),
        ],
        compiler_params=pltpu.CompilerParams(
            collective_id=0, has_side_effects=True, vmem_limit_bytes=48 << 20
        ),
        name="fused",
    )(*operands)


def solution(mesh):
    in_specs = (
        P("seq", "res"),
        P("res", "seq", None),
        P("seq", "res"),
        P("res"),
        P(),
        P(),
        P(),
        P(),
        P(),
    )
    out_specs = P("seq", "res")
    return jax.shard_map(
        on_device, mesh=mesh, in_specs=in_specs, out_specs=out_specs, check_vma=False
    )
```

time: 102 us -> 78.8 us (0.77)
  the two profiles are of different devices: /device:TPU:24 before, /device:TPU:32 now
where the time goes in v2:
time: 78.8 us; the launch traced here: 78.3 us
  Pallas kernels  71.2 us (90%)
  local copies, waits for them, and re-layouts  7.13 us (9%)
    pallas_call x1, Pallas kernels, on_device(): pl.pallas_call(fused_kernel, out_shape=jax.ShapeDtypeStruct((SEQS, RES *...  71.2 us
    unnamed x19, local copies, waits for them, and re-layouts  7.13 us

profile of v2, /device:TPU:32, one launch (start us, length us, event | category | flops | bytes accessed | tf_op | source)
XLA Modules:
  0.0 78.3 jit_solution(894578673966685204)
XLA Ops:
  0.0 0.0 copy-start.7
  0.0 0.0 copy-start.8
  0.0 0.7 copy-done.7
  0.7 0.0 copy-done.8
  0.7 0.0 copy-start
  0.7 1.2 %copy-done = bf16[32,128,128]{2,1,0:T(8,128)(2,1)S(1)} copy-done((bf16[32,128,128]{2,1,0:T(8,128)(2,1)S(1)}, bf16[32,128,128]{2,1,0:T(8,128)(2,1)}, u32[]{:S(2)}) %copy-start) | copy-done | bytes 1048600
  1.9 0.0 copy-start.1
  1.9 0.9 %copy-done.1 = bf16[32,2048]{1,0:T(8,128)(2,1)S(1)} copy-done((bf16[32,2048]{1,0:T(8,128)(2,1)S(1)}, bf16[32,2048]{1,0:T(8,128)(2,1)}, u32[]{:S(2)}) %copy-start.1) | copy-done | bytes 131096
  2.8 0.0 copy-start.2
  2.8 0.8 copy-done.2
  3.6 0.0 copy-start.3
  3.6 0.8 copy-done.3
  4.3 0.0 copy-start.4
  4.3 0.7 copy-done.4
  5.1 0.0 copy-start.5
  5.1 0.7 copy-done.5
  5.8 0.0 copy-start.6
  5.8 0.7 copy-done.6
  6.5 71.2 %fused.1 = bf16[32,2048]{1,0:T(8,128)(2,1)S(1)} custom-call(bf16[32,2048]{1,0:T(8,128)(2,1)S(1)} %copy-done.1, bf16[32,128,128]{2,1,0:T(8,128)(2,1)S(1)} %copy-done, s32[32,32]{1,0:T(8,128)S(1)} %copy-done.4, s32[1,32]{1,0:T(1,128)S(1)} %bitcast.3, bf16[8,128]{1,0:T(8,128)(2,1)S(1)} %bitcast.2, bf16[64,256]{1,0:T(8,128)(2,1)S(1)} %copy-done.2, ...), custom_call_target="tpu_custom_call" | custom-call | tf_op jit(solution)/shard_map/fused/pallas_call | solution.py:523
  77.7 0.7 copy.11
Async XLA Ops:
  0.0 0.7 copy-start.7
  0.0 0.7 copy-start.8
  0.7 1.2 %copy-start = (bf16[32,128,128]{2,1,0:T(8,128)(2,1)S(1)}, bf16[32,128,128]{2,1,0:T(8,128)(2,1)}, u32[]{:S(2)}) copy-start(bf16[32,128,128]{2,1,0:T(8,128)(2,1)} %pair_hbm.1) | copy-start | bytes 3145732
  1.9 0.9 %copy-start.1 = (bf16[32,2048]{1,0:T(8,128)(2,1)S(1)}, bf16[32,2048]{1,0:T(8,128)(2,1)}, u32[]{:S(2)}) copy-start(bf16[32,2048]{1,0:T(8,128)(2,1)} %x_hbm.1) | copy-start | bytes 393220
  2.8 0.8 copy-start.2
  3.6 0.8 copy-start.3
  4.3 0.7 copy-start.4
  5.1 0.7 copy-start.5
  5.8 0.7 copy-start.6

commit v3 on v2

--- a/solution.py
+++ b/solution.py
@@ -9,11 +9,12 @@
 F32, BF16 = jnp.float32, jnp.bfloat16
 SEQS, RES, PAIRS, LANES = 32, 32, 16, 128
 ROWS = PAIRS + SEQS * PAIRS
-GROUPS = 4
-PER_GROUP = SEQS // GROUPS
+COUNTS = (4, 8, 10, 10)
+GROUPS = len(COUNTS)
 LOG2E = 1.4426950408889634
 SPANS = [
-    (0 if g == 0 else PAIRS + g * PER_GROUP * PAIRS, PER_GROUP * PAIRS + (PAIRS if g == 0 else 0)) for g in range(GROUPS)
+    (0 if g == 0 else PAIRS * (1 + sum(COUNTS[:g])), PAIRS * (COUNTS[g] + (g == 0)))
+    for g in range(GROUPS)
 ]
 
 
@@ -43,14 +44,14 @@
     return dot(high, right) + dot(low, right)
 
 
-def normalize(values, width, coarse=False):
+def normalize(values, width):
     shape = (LANES, LANES)
     average = jnp.where(
         rows_of(shape) // width == lanes_of(shape) // width, 1.0 / width, 0.0
     ).astype(BF16)
     centre = values.astype(F32) - dot(values, average)
     squares = centre * centre
-    spread = dot(squares.astype(BF16), average) if coarse else dot_split(squares, average)
+    spread = dot_split(squares, average)
     return centre * lax.rsqrt(spread + 1e-05)
 
 
@@ -70,14 +71,12 @@
 
 
 SCHEDULE = [
-    (1, "far", 1),
-    (1, "next", 2),
-    (3, "core", 1),
-    (4, "far", 2),
-    (4, "next", 3),
-    (7, "core", 2),
-    (7, "far", 3),
-    (11, "core", 3),
+    (1, "core", 1),
+    (3, "next", 2),
+    (3, "near", 3),
+    (5, "core", 2),
+    (7, "next", 3),
+    (10, "core", 3),
 ]
 
 
@@ -113,15 +112,20 @@
     logits_odd,
     peak_even,
     peak_odd,
+    taken_even,
+    taken_odd,
+    total_even,
+    total_odd,
     kepts,
     results,
     means,
     sums,
     load_sem,
     send_sem,
+    own_send,
+    own_recv,
     z_recv,
     y_recv,
-    far_recv,
     core_recv,
     bias_send,
     bias_recv,
@@ -134,11 +138,11 @@
         pltpu.make_async_copy(source, target, load_sem.at[slot])
         for slot, (source, target) in enumerate(
             [
-                (pair_hbm, pair_ref),
-                (offset_hbm, offset_ref),
                 (x_hbm, x_ref),
                 (present_hbm, present_ref),
                 (amino_hbm, amino_ref),
+                (pair_hbm, pair_ref),
+                (offset_hbm, offset_ref),
                 (weights_hbm, weights_ref),
                 (exit_hbm, exit_ref),
                 (column_hbm, column_ref),
@@ -160,43 +164,25 @@
 
     z_peers = [place((z + d) % 4, y, core) for d in (1, 2, 3)]
     up_peer, down_peer, core_peer = place(z, up, core), place(z, down, core), place(z, y, 1 - core)
-    res_peers = z_peers + [up_peer, down_peer, core_peer]
+    across_peer = place(z, across, core)
+    res_peers = z_peers + [up_peer, down_peer, across_peer, core_peer]
     barrier = pltpu.get_barrier_semaphore()
     for peer in seq_peers:
         pl.semaphore_signal(barrier, inc=1, device_id=(peer, res), device_id_type=MESH)
     for peer in res_peers:
         pl.semaphore_signal(barrier, inc=1, device_id=(seq, peer), device_id_type=MESH)
 
-    loads[0].wait()
-    loads[1].wait()
-
-    def bias_rows(step, carry):
-        pair = pair_ref[pl.ds(step * 4, 4)].reshape(4 * LANES, LANES)
-        normed = normalize(pair, LANES, coarse=True).astype(BF16)
-        found = dot_nt(offset_ref[...], normed)
-        for row in range(4):
-            offsets[pl.ds(pl.multiple_of(step * 32 + row * 8, 8), 8), :] = found[
-                :, row * LANES : (row + 1) * LANES
-            ]
-        return carry
-
-    lax.fori_loop(0, 8, bias_rows, 0, unroll=2)
-    for head in range(8):
-        for parity in range(2):
-            biases[seq, pl.ds(head * 32 + parity * 16, 16), :] = offsets[
-                pl.ds(parity * 8 + head, 16, stride=16), :
-            ].astype(BF16)
-
     whole = (SEQS, PAIRS, LANES)
     flat = (SEQS * PAIRS, LANES)
-    for load in loads[2:5]:
+    for load in loads[0:3]:
         load.wait()
     for tile in range(PAIRS):
         lines[:, tile, :] = x_ref[:, tile * LANES : (tile + 1) * LANES].astype(F32)
     own = normalize(lines[...].reshape(flat).astype(BF16), 64).astype(BF16)
-    blocks[z, y, core, PAIRS:ROWS, :] = own
+    blocks[0, y, core, PAIRS:ROWS, :] = own
     kept = (present_ref[...] * amino_ref[...]).astype(F32).astype(BF16)
     turned = jnp.zeros((PAIRS, LANES), F32)
+    counted = jnp.zeros((PAIRS, LANES), F32)
     for parity in range(2):
         shape = (PAIRS, SEQS)
         picked = dot_nt(flag(lanes_of(shape) == 2 * rows_of(shape) + parity), kept)
@@ -204,7 +190,9 @@
         turned += dot(
             picked.astype(BF16), flag(lanes_of(shape) == rows_of(shape) + parity * SEQS)
         )
-    blocks[z, y, core, 0:PAIRS, :] = jnp.where(
+        counted += dot(picked.astype(BF16), flag(lanes_of(shape) // 64 == parity))
+    biases[seq, 256:272, :] = counted.astype(BF16)
+    blocks[0, y, core, 0:PAIRS, :] = jnp.where(
         lanes_of((PAIRS, LANES)) < 64, 1000000000.0 * (turned - 1.0), 1.0
     ).astype(BF16)
 
@@ -218,68 +206,69 @@
             device_id_type=MESH,
         )
 
-    def one(z_at, group):
-        return blocks.at[z_at, y, core, pl.ds(*SPANS[group]), :]
-
     def column(y_at, core_at, group, first=0, count=4):
         return blocks.at[pl.ds(first, count), y_at, core_at, pl.ds(*SPANS[group]), :]
 
     def z_copy(group, d):
-        return remote(one(z, group), send_sem.at[group, d - 1], z_recv.at[z, group], z_peers[d - 1])
-
-    def z_wait(group, d):
-        at = (z + d) % 4
-        remote(one(at, group), send_sem.at[group, 0], z_recv.at[at, group], res).wait_recv()
+        rows = pl.ds(*SPANS[group])
+        return pltpu.make_async_remote_copy(
+            src_ref=blocks.at[0, y, core, rows, :],
+            dst_ref=blocks.at[4 - d, y, core, rows, :],
+            send_sem=send_sem.at[group, d - 1],
+            recv_sem=z_recv.at[4 - d, group],
+            device_id=(seq, z_peers[d - 1]),
+            device_id_type=MESH,
+        )
+
+    def own_copy(side, source):
+        target = (up_peer, down_peer, across_peer, core_peer)[side]
+        return remote(
+            blocks.at[0, source, core] if side < 3 else blocks.at[0, y, source],
+            own_send.at[side],
+            own_recv.at[(1, 0, 2, 3)[side]],
+            target,
+        )
 
     def y_copy(group, side, source):
-        target = (up_peer, down_peer)[side]
+        target = (up_peer, down_peer, across_peer)[side]
         return remote(
-            column(source, core, group),
+            column(source, core, group, 1, 3),
             send_sem.at[group, 3 + side],
-            y_recv.at[1 - side, group],
+            y_recv.at[(1, 0, 2)[side], group],
             target,
         )
 
-    def far_copy(group, side, source):
-        target = (up_peer, down_peer)[side]
+    def core_copy(group, slot, source, core_at):
+        first = 1 if slot == 0 else 0
         return remote(
-            column(source, core, group, 2 * side, 2),
-            send_sem.at[group, 5 + side],
-            far_recv.at[side, group],
-            target,
-        )
-
-    def core_copy(group, slot, source, core_at):
-        return remote(
-            column(source, core_at, group),
-            send_sem.at[group, 7 + slot],
-            core_recv.at[source, group],
+            column(source, core_at, group, first, 4 - first),
+            send_sem.at[group, 6 + slot],
+            core_recv.at[slot, group],
             core_peer,
         )
 
     def stage_near(group):
         for d in (1, 2, 3):
-            z_wait(group, d)
-        y_copy(group, 0, y).start()
-        y_copy(group, 1, y).start()
+            z_copy(group, d).wait_recv()
+        if group + 1 < GROUPS:
+            for d in (1, 2, 3):
+                z_copy(group + 1, d).start()
+        for side in range(3):
+            y_copy(group, side, y).start()
         core_copy(group, 0, y, core).start()
 
     def stage_next(group):
-        y_copy(group, 0, down).wait_recv()
-        far_copy(group, 0, down).start()
-        core_copy(group, 1, down, core).start()
-        y_copy(group, 1, up).wait_recv()
-        far_copy(group, 1, up).start()
-        core_copy(group, 2, up, core).start()
-
-    def stage_far(group):
-        far_copy(group, 0, across).wait_recv()
-        far_copy(group, 1, across).wait_recv()
-        core_copy(group, 3, across, core).start()
+        for side, source in enumerate((down, up, across)):
+            if group == 0:
+                own_copy(side, source).wait_recv()
+            y_copy(group, side, source).wait_recv()
+            core_copy(group, side + 1, source, core).start()
 
     def stage_core(group):
-        for at in range(4):
-            core_copy(group, 0, at, 1 - core).wait_recv()
+        if group == 0:
+            own_copy(3, 1 - core).wait_recv()
+        for slot, at in enumerate((y, down, up, across)):
+            core_copy(group, slot, at, 1 - core).wait_recv()
 
     def bias_copy(block, slot, target):
         return pltpu.make_async_remote_copy(
@@ -292,13 +281,44 @@
         )
 
     pl.semaphore_wait(barrier, len(seq_peers) + len(res_peers))
+    for side in range(3):
+        own_copy(side, y).start()
     for d in (1, 2, 3):
         z_copy(0, d).start()
+    own_copy(3, core).start()
+
+    for load in loads[3:5]:
+        load.wait()
+
+    shape = (256, 256)
+    average = jnp.where(
+        rows_of(shape) // LANES == lanes_of(shape) // LANES, 1.0 / LANES, 0.0
+    ).astype(BF16)
+
+    def bias_rows(step, carry):
+        pair = pair_ref[pl.ds(step * 4, 4)].reshape(4 * LANES, LANES)
+        pair = jnp.concatenate([pair[:256], pair[256:]], axis=1)
+        centre = pair.astype(F32) - dot(pair, average)
+        spread = dot((centre * centre).astype(BF16), average)
+        normed = (centre * lax.rsqrt(spread + 1e-05)).astype(BF16)
+        for row in range(4):
+            start = row // 2 * LANES
+            found = dot_nt(
+                offset_ref[...],
+                normed[row % 2 * LANES : row % 2 * LANES + LANES, start : start + LANES],
+            )
+            offsets[pl.ds(pl.multiple_of(step * 32 + row * 8, 8), 8), :] = found
+        return carry
+
+    lax.fori_loop(0, 8, bias_rows, 0, unroll=2)
+    for head in range(8):
+        for parity in range(2):
+            biases[seq, pl.ds(head * 32 + parity * 16, 16), :] = offsets[
+                pl.ds(parity * 8 + head, 16, stride=16), :
+            ].astype(BF16)
+
     for slot, peer in enumerate(bias_peers):
         bias_copy(seq, slot, peer).start()
-    for group in range(1, GROUPS):
-        for d in (1, 2, 3):
-            z_copy(group, d).start()
 
     for load in loads[5:]:
         load.wait()
@@ -330,37 +350,36 @@
                     :, parity * LANES : (parity + 1) * LANES
                 ].reshape(whole)
 
+    stage_near(0)
     query_side(0)
-    stage_near(0)
     query_side(1)
-    stage_near(1)
+    stage_next(0)
     bias_copy(partner, 0, seq).wait_recv()
     for slot, peer in enumerate(bias_peers[1:]):
         bias_copy(partner, 4 + slot, peer).start()
+    stage_near(1)
 
     spread = (RES, RES * 64)
     kept = dot(kept, flag(rows_of(spread) == lanes_of(spread) // 64))
     for tile in range(PAIRS):
         kepts[:, tile, :] = kept[:, tile * LANES : (tile + 1) * LANES]
 
-    stage_next(0)
-    stage_near(2)
-    stage_far(0)
-    stage_near(3)
-    stage_next(1)
     for peer in bias_peers[1:]:
         bias_copy(peer, 0, seq).wait_recv()
         bias_copy(peer // 2 * 2 + (1 - peer % 2), 0, seq).wait_recv()
     shape = (256, 256)
     order = flag(rows_of(shape) == 2 * (lanes_of(shape) % LANES) + lanes_of(shape) // LANES)
     for tile in range(4):
-        both = jnp.concatenate([biases[2 * tile], biases[2 * tile + 1]], axis=1)
+        at = (z + tile) % 4
+        both = jnp.concatenate([biases[2 * at, 0:256], biases[2 * at + 1, 0:256]], axis=1)
         placed = dot(both, order) * LOG2E
         for parity in range(2):
             bias[parity * 256 : parity * 256 + 256, tile * LANES : (tile + 1) * LANES] = placed[
                 :, parity * LANES : (parity + 1) * LANES
             ]
     stage_core(0)
+    stage_next(1)
+    stage_near(2)
 
     value_weights = jnp.where(lane >= 64, tile_rows(weights, 128), 0.0).astype(BF16)
     half = lanes_of((256, LANES)) < 64
@@ -385,19 +404,22 @@
         peak = jnp.max(jnp.maximum(peak[:256], peak[256:]), axis=1, keepdims=True)
         peak_ref[...] = jnp.broadcast_to(peak, (256, LANES))
 
-    def weigh(line, logits_ref, peak_ref):
+    def weigh(line, logits_ref, peak_ref, taken_ref, total_ref):
         peak = jnp.concatenate([peak_ref[...]] * 4, axis=1)
         peak = jnp.concatenate([peak, peak], axis=0)
         exped = jnp.exp2(logits_ref[...] - peak).astype(BF16)
         summed = dot(exped, keys_of(line))
-        taken = jnp.where(half, summed[:256, :LANES], summed[256:, :LANES]).astype(BF16)
-        total = summed[:256, LANES:] + summed[256:, LANES:]
-        found = dot(taken, value_weights) / total
+        taken_ref[...] = jnp.where(half, summed[:256, :LANES], summed[256:, :LANES]).astype(BF16)
+        total_ref[...] = summed[:256, LANES:] + summed[256:, LANES:]
+
+    def finish(line, taken_ref, total_ref):
+        found = dot(taken_ref[...], value_weights) / total_ref[...]
         attended = jnp.zeros((32, LANES), F32)
         for head in range(8):
             attended = jnp.where(head_of == head, found[head * 32 : head * 32 + 32], attended)
         gateds[line] = (gates[line] * attended).astype(BF16)
 
+    stages = {"near": stage_near, "next": stage_next, "core": stage_core}
     score(0, logits_even, peak_even)
 
     def two_lines(step, carry):
@@ -405,16 +427,21 @@
 
             @pl.when(step == at)
             def _():
-                {"next": stage_next, "far": stage_far, "core": stage_core}[stage](group)
+                stages[stage](group)
 
         line = 2 * step
         score(line + 1, logits_odd, peak_odd)
-        weigh(line, logits_even, peak_even)
+        weigh(line, logits_even, peak_even, taken_even, total_even)
+        finish(jnp.maximum(line - 1, 0), taken_odd, total_odd)
         score(jnp.minimum(line + 2, SEQS - 1), logits_even, peak_even)
-        weigh(line + 1, logits_odd, peak_odd)
+        weigh(line + 1, logits_odd, peak_odd, taken_odd, total_odd)
+        finish(line, taken_even, total_even)
         return carry
 
+    taken_odd[...] = jnp.zeros((256, LANES), BF16)
+    total_odd[...] = jnp.ones((256, LANES), F32)
     lax.fori_loop(0, SEQS // 2, two_lines, 0)
+    finish(SEQS - 1, taken_odd, total_odd)
 
     exits = tile_rows(exit_ref[...], 0)
     update = jnp.zeros(flat, F32)
@@ -424,25 +451,20 @@
     line = (lines[...].reshape(flat) + update).astype(BF16)
     normed = normalize(line, 64).astype(BF16)
 
-    def exchange(buffer, send, recv):
-        def copy(source, slot, target):
-            return pltpu.make_async_remote_copy(
-                src_ref=buffer.at[source],
-                dst_ref=buffer.at[source],
-                send_sem=send.at[slot],
-                recv_sem=recv.at[source],
-                device_id=(target, res),
-                device_id_type=MESH,
-            )
-
-        for slot, peer in enumerate(seq_peers):
-            copy(seq, slot, peer).start()
-        return copy
+    def share(buffer, send, recv, d):
+        return pltpu.make_async_remote_copy(
+            src_ref=buffer.at[0],
+            dst_ref=buffer.at[8 - d],
+            send_sem=send.at[d],
+            recv_sem=recv.at[8 - d],
+            device_id=(seq_peers[d - 1], res),
+            device_id_type=MESH,
+        )
 
     kept = kepts[...]
-    means[seq, 0:16, :] = jnp.sum(kept * normed.astype(F32).reshape(whole), axis=0)
-    means[seq, 16:32, :] = jnp.sum(kept, axis=0)
-    mean_copy = exchange(means, mean_send, mean_recv)
+    means[0] = jnp.sum(kept * normed.astype(F32).reshape(whole), axis=0).astype(BF16)
+    for d in range(1, 8):
+        share(means, mean_send, mean_recv, d).start()
 
     weights = column_ref[...]
     gate = jax.nn.sigmoid(dot(normed, twice(weights, 64)))
@@ -457,26 +479,32 @@
     value = dot(normed, value_weights).reshape(whole)
     head_sum = flag(row // 8 == lane // 8)
 
-    for slot, peer in enumerate(seq_peers):
-        mean_copy(peer, slot, seq).wait_recv()
-    total = jnp.sum(means[...], axis=0)
-    mean = total[:16] / jnp.maximum(total[16:], 1.0)
+    count = jnp.sum(biases[:, 256:272, :].astype(F32), axis=0)
+    for d in range(1, 8):
+        share(means, mean_send, mean_recv, d).wait_recv()
+    mean = jnp.sum(means[...].astype(F32), axis=0) / jnp.maximum(count, 1.0)
     mean_query = dot_split(mean, query_weights) * 8**-0.5
     logits = dot_split((key * mean_query[None]).reshape(flat), head_sum).reshape(whole)
     logits = logits + 1000000000.0 * (kept - 1.0)
     peak = jnp.max(logits, axis=0)
     exped = jnp.exp(logits - peak[None])
-    sums[seq, 0:16, :] = peak
-    sums[seq, 16:32, :] = jnp.sum(exped, axis=0)
-    sums[seq, 32:48, :] = jnp.sum(exped * value, axis=0)
-    sum_copy = exchange(sums, sum_send, sum_recv)
-    for slot, peer in enumerate(seq_peers):
-        sum_copy(peer, slot, seq).wait_recv()
-    peaks = sums[:, 0:16, :]
-    factor = jnp.exp(peaks - jnp.max(peaks, axis=0)[None])
-    attended = jnp.sum(factor * sums[:, 32:48, :], axis=0) / jnp.sum(
-        factor * sums[:, 16:32, :], axis=0
-    )
+    total = jnp.sum(exped, axis=0)
+    sums[0, 0:16, :] = (jnp.sum(exped * value, axis=0) / total).astype(BF16)
+    weight = peak + jnp.log(total)
+    part = lanes_of((PAIRS, LANES)) % 8
+    terms = jnp.zeros((PAIRS, LANES), BF16)
+    for term in range(3):
+        rounded = weight.astype(BF16)
+        terms = jnp.where(part == term, rounded.astype(F32), terms.astype(F32)).astype(BF16)
+        weight = weight - rounded.astype(F32)
+    sums[0, 16:32, :] = terms
+    for d in range(1, 8):
+        share(sums, sum_send, sum_recv, d).start()
+    for d in range(1, 8):
+        share(sums, sum_send, sum_recv, d).wait_recv()
+    weight = dot(sums[:, 16:32, :].reshape(8 * PAIRS, LANES), head_sum).reshape(8, PAIRS, LANES)
+    factor = jnp.exp(weight - jnp.max(weight, axis=0)[None])
+    attended = jnp.sum(factor * sums[:, 0:16, :].astype(F32), axis=0) / jnp.sum(factor, axis=0)
     gated = (gate.reshape(whole) * attended[None]).astype(BF16).reshape(flat)
     final = line.astype(F32) + dot(gated, twice(exit_col_ref[...], 0))
     results[...] = final.reshape(whole)
@@ -485,14 +513,16 @@
 
     for slot in range(7):
         bias_copy(seq, slot, seq).wait_send()
-        mean_copy(seq, slot, seq).wait_send()
-        sum_copy(seq, slot, seq).wait_send()
+    for d in range(1, 8):
+        share(means, mean_send, mean_recv, d).wait_send()
+        share(sums, sum_send, sum_recv, d).wait_send()
+    for side, source in enumerate((y, y, y, core)):
+        own_copy(side, source).wait_send()
     for group in range(GROUPS):
         for d in (1, 2, 3):
             z_copy(group, d).wait_send()
-        for side in range(2):
+        for side in range(3):
             y_copy(group, side, y).wait_send()
-            far_copy(group, side, y).wait_send()
         for slot in range(4):
             core_copy(group, slot, y, core).wait_send()
 
@@ -528,7 +558,7 @@
         scratch_shapes=[vmem(operand.shape, operand.dtype) for operand in operands]
         + [
             vmem((4, 4, 2, ROWS, LANES), BF16),
-            vmem((8, 256, LANES), BF16),
+            vmem((8, 272, LANES), BF16),
             vmem((SEQS, PAIRS, LANES), F32),
             vmem((256, LANES), F32),
             vmem((512, 512), F32),
@@ -539,25 +569,30 @@
             vmem((512, 512), F32),
             vmem((256, LANES), F32),
             vmem((256, LANES), F32),
+            vmem((256, LANES), BF16),
+            vmem((256, LANES), BF16),
+            vmem((256, LANES), F32),
+            vmem((256, LANES), F32),
             vmem((SEQS, PAIRS, LANES), F32),
             vmem((SEQS, PAIRS, LANES), F32),
-            vmem((8, 32, LANES), F32),
-            vmem((8, 48, LANES), F32),
+            vmem((8, PAIRS, LANES), BF16),
+            vmem((8, 32, LANES), BF16),
             dma((len(operands),)),
-            dma((GROUPS, 11)),
+            dma((GROUPS, 10)),
+            dma((4,)),
+            dma((4,)),
             dma((4, GROUPS)),
-            dma((2, GROUPS)),
-            dma((2, GROUPS)),
+            dma((3, GROUPS)),
             dma((4, GROUPS)),
             dma((7,)),
             dma((8,)),
-            dma((7,)),
             dma((8,)),
-            dma((7,)),
+            dma((8,)),
+            dma((8,)),
             dma((8,)),
         ],
         compiler_params=pltpu.CompilerParams(
-            collective_id=0, has_side_effects=True, vmem_limit_bytes=48 << 20
+            collective_id=0, has_side_effects=True, vmem_limit_bytes=60 << 20
         ),
         name="fused",
     )(*operands)

time: 78.8 us -> 68.6 us (0.87)
  local copies, waits for them, and re-layouts: 7.13 us -> 1.57 us
  Pallas kernels: 71.2 us -> 66.9 us
    unnamed x19 -> x1, local copies, waits for them, and re-layouts: 7.13 us -> 1.57 us
    pallas_call x1, Pallas kernels: 71.2 us -> 66.9 us  [on_device(): pl.pallas_call(fused_kernel, out_shape=jax.ShapeDtypeStruct((SEQS, RES *...]
where the time goes in v3:
time: 68.6 us; the launch traced here: 68.5 us
  Pallas kernels  66.9 us (98%)
  local copies, waits for them, and re-layouts  1.57 us (2%)
    pallas_call x1, Pallas kernels, on_device(): pl.pallas_call(fused_kernel, out_shape=jax.ShapeDtypeStruct((SEQS, RES *...  66.9 us
    unnamed x1, local copies, waits for them, and re-layouts  1.57 us

profile of v3, /device:TPU:32, one launch (start us, length us, event | category | flops | bytes accessed | tf_op | source)
XLA Modules:
  0.0 68.5 jit_solution(5646313910117890668)
XLA Ops:
  0.0 66.9 %fused.1 = bf16[32,2048]{1,0:T(8,128)(2,1)} custom-call(bf16[32,2048]{1,0:T(8,128)(2,1)} %x_hbm.1, bf16[32,128,128]{2,1,0:T(8,128)(2,1)} %pair_hbm.1, s32[32,32]{1,0:T(8,128)} %present_hbm.1, s32[1,32]{1,0:T(1,128)} %bitcast.3, bf16[8,128]{1,0:T(8,128)(2,1)} %bitcast.2, bf16[64,256]{1,0:T(8,128)(2,1)} %weights_hbm.1, bf16[64,64]{1,0:T(8,128)(2,1)} %exit_hbm.1, ...), custom_call_target="tpu_custom_call" | custom-call | tf_op jit(solution)/shard_map/fused/pallas_call | solution.py:553
  66.9 1.6 %copy.11 = bf16[32,2048]{1,0:T(8,128)(2,1)} copy(bf16[32,2048]{1,0:T(8,128)(2,1)} %fused.1) | data formatting | bytes 262144

commit v4 on v3

--- a/solution.py
+++ b/solution.py
@@ -72,11 +72,11 @@
 
 SCHEDULE = [
     (1, "core", 1),
-    (3, "next", 2),
-    (3, "near", 3),
-    (5, "core", 2),
-    (7, "next", 3),
-    (10, "core", 3),
+    (2, 'near', 3),
+    (3, 'next', 2),
+    (5, 'core', 2),
+    (6, 'next', 3),
+    (10, 'core', 3),
 ]
 
 

time: 68.6 us -> 66.8 us (0.974)
  Pallas kernels: 66.9 us -> 65 us
    pallas_call x1, Pallas kernels: 66.9 us -> 65 us  [on_device(): pl.pallas_call(fused_kernel, out_shape=jax.ShapeDtypeStruct((SEQS, RES *...]
where the time goes in v4:
time: 66.8 us; the launch traced here: 66.6 us
  Pallas kernels  65 us (97%)
  local copies, waits for them, and re-layouts  1.57 us (2%)
    pallas_call x1, Pallas kernels, on_device(): pl.pallas_call(fused_kernel, out_shape=jax.ShapeDtypeStruct((SEQS, RES *...  65 us
    unnamed x1, local copies, waits for them, and re-layouts  1.57 us

profile of v4, /device:TPU:32, one launch (start us, length us, event | category | flops | bytes accessed | tf_op | source)
XLA Modules:
  0.0 66.6 jit_solution(14279062023549269637)
XLA Ops:
  0.0 65.0 %fused.1 = bf16[32,2048]{1,0:T(8,128)(2,1)} custom-call(bf16[32,2048]{1,0:T(8,128)(2,1)} %x_hbm.1, bf16[32,128,128]{2,1,0:T(8,128)(2,1)} %pair_hbm.1, s32[32,32]{1,0:T(8,128)} %present_hbm.1, s32[1,32]{1,0:T(1,128)} %bitcast.3, bf16[8,128]{1,0:T(8,128)(2,1)} %bitcast.2, bf16[64,256]{1,0:T(8,128)(2,1)} %weights_hbm.1, bf16[64,64]{1,0:T(8,128)(2,1)} %exit_hbm.1, ...), custom_call_target="tpu_custom_call" | custom-call | tf_op jit(solution)/shard_map/fused/pallas_call | solution.py:553
  65.0 1.6 %copy.11 = bf16[32,2048]{1,0:T(8,128)(2,1)} copy(bf16[32,2048]{1,0:T(8,128)(2,1)} %fused.1) | data formatting | bytes 262144

commit v5 on v4

--- a/solution.py
+++ b/solution.py
@@ -9,7 +9,7 @@
 F32, BF16 = jnp.float32, jnp.bfloat16
 SEQS, RES, PAIRS, LANES = 32, 32, 16, 128
 ROWS = PAIRS + SEQS * PAIRS
-COUNTS = (4, 8, 10, 10)
+COUNTS = (4, 8, 12, 8)
 GROUPS = len(COUNTS)
 LOG2E = 1.4426950408889634
 SPANS = [
@@ -76,7 +76,7 @@
     (3, 'next', 2),
     (5, 'core', 2),
     (6, 'next', 3),
-    (10, 'core', 3),
+    (11, "core", 3),
 ]
 
 

time: 66.8 us -> 67 us (level)
  no operation moved by 1% of the time
where the time goes in v5:
time: 67 us; the launch traced here: 66.8 us
  Pallas kernels  65.2 us (97%)
  local copies, waits for them, and re-layouts  1.57 us (2%)
    pallas_call x1, Pallas kernels, on_device(): pl.pallas_call(fused_kernel, out_shape=jax.ShapeDtypeStruct((SEQS, RES *...  65.2 us
    unnamed x1, local copies, waits for them, and re-layouts  1.57 us

profile of v5, /device:TPU:32, one launch (start us, length us, event | category | flops | bytes accessed | tf_op | source)
XLA Modules:
  0.0 66.8 jit_solution(1384565135124547528)
XLA Ops:
  0.0 65.2 %fused.1 = bf16[32,2048]{1,0:T(8,128)(2,1)} custom-call(bf16[32,2048]{1,0:T(8,128)(2,1)} %x_hbm.1, bf16[32,128,128]{2,1,0:T(8,128)(2,1)} %pair_hbm.1, s32[32,32]{1,0:T(8,128)} %present_hbm.1, s32[1,32]{1,0:T(1,128)} %bitcast.3, bf16[8,128]{1,0:T(8,128)(2,1)} %bitcast.2, bf16[64,256]{1,0:T(8,128)(2,1)} %weights_hbm.1, bf16[64,64]{1,0:T(8,128)(2,1)} %exit_hbm.1, ...), custom_call_target="tpu_custom_call" | custom-call | tf_op jit(solution)/shard_map/fused/pallas_call | solution.py:553
  65.2 1.6 %copy.11 = bf16[32,2048]{1,0:T(8,128)(2,1)} copy(bf16[32,2048]{1,0:T(8,128)(2,1)} %fused.1) | data formatting | bytes 262144
